TPU v7x, 32 devices: a whole 2x2x4 slice. The times are simulated.
32 devices in a mesh: dp: 8 (over z, y), tensor: 4 (over x, core).
Axes of the slice: x: 2, y: 2, z: 4, core: 2. Of those that a mesh axis runs over, the one named last changes fastest.
Arguments:
- hidden_in: bfloat16 [8192, 1024], P(('dp', 'tensor')), may hold values from -11 to 11
- out_grad: bfloat16 [8192, 1024], P(('dp', 'tensor')), may hold values from -6 to 6
- prefix_len: int32 [8], P('dp'), may hold values from 102 to 512
- qkv_weight: bfloat16 [1024, 3072], P(None, 'tensor'), may hold values from -1 to 1
- qv_bias: float32 [16, 2, 64], P('tensor'), may hold values from -1.8 to 1.8
- dense_weight: bfloat16 [1024, 1024], P('tensor'), may hold values from -0.5 to 0.5
- dense_bias: float32 [1024], replicated, may hold values from -1.8 to 1.8
- norm1_gain: float32 [1024], replicated, may hold values from 0.25 to 1.75
- norm1_shift: float32 [1024], replicated, may hold values from -1.8 to 1.8
- norm2_gain: float32 [1024], replicated, may hold values from 0.25 to 1.75
- norm2_shift: float32 [1024], replicated, may hold values from -1.8 to 1.8
- fc1_weight: bfloat16 [1024, 4096], P(None, 'tensor'), may hold values from -1 to 1
- fc1_bias: float32 [4096], P('tensor'), may hold values from -1.8 to 1.8
- fc2_weight: bfloat16 [4096, 1024], P('tensor'), may hold values from -0.1875 to 0.1875
- fc2_bias: float32 [1024], replicated, may hold values from -1.8 to 1.8
Outputs:
- hidden_out: bfloat16 [8192, 1024], P(('dp', 'tensor'))
- hidden_grad: bfloat16 [8192, 1024], P(('dp', 'tensor'))
- qkv_weight_grad: float32 [1024, 3072], P(None, 'tensor')
- qv_bias_grad: float32 [16, 2, 64], P('tensor')
- dense_weight_grad: float32 [1024, 1024], P('tensor')
- dense_bias_grad: float32 [1024], replicated
- norm1_gain_grad: float32 [1024], replicated
- norm1_shift_grad: float32 [1024], replicated
- norm2_gain_grad: float32 [1024], replicated
- norm2_shift_grad: float32 [1024], replicated
- fc1_weight_grad: float32 [1024, 4096], P(None, 'tensor')
- fc1_bias_grad: float32 [4096], P('tensor')
- fc2_weight_grad: float32 [4096, 1024], P('tensor')
- fc2_bias_grad: float32 [1024], replicated
- sublayer_rms: float32 [4], replicated
All inputs are finite; a program needn't handle non-finite values.
Results may differ from a plain program's by a relative error of at most 0.015.
Values may be sent and summed in bfloat16 or wider, within the bound.
No kernel may reach another device: no remote copies, remote signals or barrier semaphores. Data moves between devices by JAX's collectives and lax.ppermute only.
A program may use at most 128 MiB of HBM per device.

v0:
```python
from functools import partial

import jax
import jax.numpy as jnp
from jax import lax
from jax.sharding import PartitionSpec as P

HEADS = 16


epsilon = 1e-05
masked_value = -1e30


def layer_norm(values, gain, shift):
    center = jnp.mean(values, axis=-1, keepdims=True)
    deviation = values - center
    variance = jnp.mean(deviation * deviation, axis=-1, keepdims=True)
    return deviation * lax.rsqrt(variance + epsilon) * gain + shift


def norm_backward(values, gain, shift, upstream):
    _, pullback = jax.vjp(layer_norm, values, gain, shift)
    return pullback(upstream)


def contract_rows(left_op, right_op):
    return lax.dot_general(
        left_op, right_op, (((0,), (0,)), ((), ())), preferred_element_type=jnp.float32
    )


def contract_cols(left_op, right_op):
    return lax.dot_general(
        left_op, right_op, (((1,), (1,)), ((), ())), preferred_element_type=jnp.float32
    )


def block_scores(query_block, key_rows, first_row, prefix, slopes, score_scale):
    row_count = query_block.shape[0]
    length = key_rows.shape[0]
    row_pos = first_row + lax.iota(jnp.int32, row_count)[:, None]
    col_pos = lax.iota(jnp.int32, length)[None, :]
    allowed = (col_pos <= row_pos) | (col_pos < prefix) & (row_pos < prefix)
    distance = jnp.abs(row_pos - col_pos).astype(jnp.float32)
    scores = (
        jnp.einsum("qhc,khc->hqk", query_block, key_rows, preferred_element_type=jnp.float32)
        * score_scale
    )
    scores = scores - slopes[:, None, None] * distance[None, :, :]
    return jnp.where(allowed[None, :, :], scores, masked_value)


def attend_forward(joined, prefix, slopes, score_scale):
    length = joined.shape[0]
    block_rows = min(512, length)
    queries = joined[:, :, 0, :]
    key_rows = joined[:, :, 1, :]
    value_rows = joined[:, :, 2, :]

    def one_block(first_row):
        query_block = lax.dynamic_slice_in_dim(queries, first_row, block_rows, 0)
        scores = block_scores(query_block, key_rows, first_row, prefix, slopes, score_scale)
        highest = jnp.max(scores, axis=-1, keepdims=True)
        powered = jnp.exp(scores - highest)
        totals = jnp.sum(powered, axis=-1, keepdims=True)
        weights = (powered / totals).astype(jnp.bfloat16)
        context = jnp.einsum(
            "hqk,khc->qhc", weights, value_rows, preferred_element_type=jnp.float32
        )
        return (context.astype(jnp.bfloat16), (highest + jnp.log(totals))[:, :, 0])

    starts = jnp.arange(length // block_rows, dtype=jnp.int32) * block_rows
    context, log_totals = lax.map(one_block, starts)
    return (context.reshape(length, -1), log_totals)


def attend_backward(joined, log_totals, context_grad, prefix, slopes, score_scale):
    length = joined.shape[0]
    heads_here = joined.shape[1]
    head_size = joined.shape[3]
    block_rows = log_totals.shape[2]
    queries = joined[:, :, 0, :]
    key_rows = joined[:, :, 1, :]
    value_rows = joined[:, :, 2, :]
    grad_heads = context_grad.reshape(length, heads_here, head_size)

    def one_block(carry, item):
        key_grad, value_grad = carry
        first_row, log_block = item
        query_block = lax.dynamic_slice_in_dim(queries, first_row, block_rows, 0)
        grad_block = lax.dynamic_slice_in_dim(grad_heads, first_row, block_rows, 0)
        scores = block_scores(query_block, key_rows, first_row, prefix, slopes, score_scale)
        weights = jnp.exp(scores - log_block[:, :, None])
        weight_grad = jnp.einsum(
            "qhc,khc->hqk", grad_block, value_rows, preferred_element_type=jnp.float32
        )
        inner = jnp.sum(weights * weight_grad, axis=-1, keepdims=True)
        score_grad = (weights * (weight_grad - inner)).astype(jnp.bfloat16)
        query_grad = (
            jnp.einsum("hqk,khc->qhc", score_grad, key_rows, preferred_element_type=jnp.float32)
            * score_scale
        )
        key_grad = (
            key_grad
            + jnp.einsum(
                "hqk,qhc->khc", score_grad, query_block, preferred_element_type=jnp.float32
            )
            * score_scale
        )
        value_grad = value_grad + jnp.einsum(
            "hqk,qhc->khc",
            weights.astype(jnp.bfloat16),
            grad_block,
            preferred_element_type=jnp.float32,
        )
        return ((key_grad, value_grad), query_grad)

    zeros_grad = jnp.zeros((length, heads_here, head_size), jnp.float32)
    starts = jnp.arange(length // block_rows, dtype=jnp.int32) * block_rows
    (key_grad, value_grad), query_grad = lax.scan(
        one_block, (zeros_grad, zeros_grad), (starts, log_totals)
    )
    query_grad = query_grad.reshape(length, heads_here, head_size)
    return jnp.stack([query_grad, key_grad, value_grad], axis=2)


def local(
    hidden_in,
    out_grad,
    prefix_len,
    qkv_weight,
    qv_bias,
    dense_weight,
    dense_bias,
    norm1_gain,
    norm1_shift,
    norm2_gain,
    norm2_shift,
    fc1_weight,
    fc1_bias,
    fc2_weight,
    fc2_bias,
):
    rows_here = hidden_in.shape[0]
    features = hidden_in.shape[1]
    heads_here = qv_bias.shape[0]
    head_size = qv_bias.shape[2]
    score_scale = head_size ** (-0.5)
    head_first = lax.axis_index("tensor") * heads_here
    slopes = 2.0 ** (
        -8.0 * (head_first + 1 + lax.iota(jnp.int32, heads_here)).astype(jnp.float32) / HEADS
    )
    prefix = prefix_len[0]
    residual = hidden_in.astype(jnp.float32)
    normed1 = layer_norm(residual, norm1_gain, norm1_shift).astype(jnp.bfloat16)
    normed1_all = lax.all_gather(normed1, "tensor", axis=0, tiled=True)
    length = normed1_all.shape[0]
    bias_full = jnp.stack(
        [qv_bias[:, 0], jnp.zeros_like(qv_bias[:, 0]), qv_bias[:, 1]], axis=1
    ).reshape(-1)
    joined = (
        jnp.dot(normed1_all, qkv_weight, preferred_element_type=jnp.float32) + bias_full
    ).astype(jnp.bfloat16)
    joined = joined.reshape(length, heads_here, 3, head_size)
    context, log_totals = attend_forward(joined, prefix, slopes, score_scale)
    attn_out = (
        lax.psum_scatter(
            jnp.dot(context, dense_weight, preferred_element_type=jnp.float32),
            "tensor",
            scatter_dimension=0,
            tiled=True,
        )
        + dense_bias
    )
    middle = residual + attn_out
    normed2 = layer_norm(middle, norm2_gain, norm2_shift).astype(jnp.bfloat16)
    normed2_all = lax.all_gather(normed2, "tensor", axis=0, tiled=True)
    hidden_pre = jnp.dot(normed2_all, fc1_weight, preferred_element_type=jnp.float32) + fc1_bias
    activated = jax.nn.gelu(hidden_pre, approximate=True).astype(jnp.bfloat16)
    mlp_out = (
        lax.psum_scatter(
            jnp.dot(activated, fc2_weight, preferred_element_type=jnp.float32).astype(jnp.bfloat16),
            "tensor",
            scatter_dimension=0,
            tiled=True,
        ).astype(jnp.float32)
        + fc2_bias
    )
    final = middle + mlp_out
    squares = jnp.stack(
        [
            jnp.sum(residual * residual),
            jnp.sum(attn_out * attn_out),
            jnp.sum(mlp_out * mlp_out),
            jnp.sum(final * final),
        ]
    )
    totals_sq = lax.psum(squares, ("dp", "tensor"))
    grad_all = lax.all_gather(out_grad, "tensor", axis=0, tiled=True)
    fc2_weight_grad = contract_rows(activated, grad_all)
    act_grad = contract_cols(grad_all, fc2_weight)
    _, gelu_pull = jax.vjp(partial(jax.nn.gelu, approximate=True), hidden_pre)
    pre_grad = gelu_pull(act_grad)[0].astype(jnp.bfloat16)
    fc1_bias_grad = jnp.sum(pre_grad, axis=0, dtype=jnp.float32)
    fc1_weight_grad = contract_rows(normed2_all, pre_grad)
    normed2_grad = lax.psum_scatter(
        contract_cols(pre_grad, fc1_weight), "tensor", scatter_dimension=0, tiled=True
    )
    out_grad_full = out_grad.astype(jnp.float32)
    middle_norm_grad, norm2_gain_grad, norm2_shift_grad = norm_backward(
        middle, norm2_gain, norm2_shift, normed2_grad
    )
    middle_grad = out_grad_full + middle_norm_grad
    fc2_bias_grad = jnp.sum(out_grad_full, axis=0)
    dense_bias_grad = jnp.sum(middle_grad, axis=0)
    middle_all = lax.all_gather(middle_grad.astype(jnp.bfloat16), "tensor", axis=0, tiled=True)
    dense_weight_grad = contract_rows(context, middle_all)
    context_grad = contract_cols(middle_all, dense_weight).astype(jnp.bfloat16)
    joined_grad = attend_backward(
        joined, log_totals, context_grad, prefix, slopes, score_scale
    ).astype(jnp.bfloat16)
    qv_bias_grad = jnp.stack(
        [
            jnp.sum(joined_grad[:, :, 0, :], axis=0, dtype=jnp.float32),
            jnp.sum(joined_grad[:, :, 2, :], axis=0, dtype=jnp.float32),
        ],
        axis=1,
    )
    joined_flat = joined_grad.reshape(length, -1)
    qkv_weight_grad = contract_rows(normed1_all, joined_flat)
    normed1_grad = lax.psum_scatter(
        contract_cols(joined_flat, qkv_weight).astype(jnp.bfloat16),
        "tensor",
        scatter_dimension=0,
        tiled=True,
    ).astype(jnp.float32)
    input_norm_grad, norm1_gain_grad, norm1_shift_grad = norm_backward(
        residual, norm1_gain, norm1_shift, normed1_grad
    )
    hidden_grad = (middle_grad + input_norm_grad).astype(jnp.bfloat16)
    (
        qkv_weight_grad,
        qv_bias_grad,
        dense_weight_grad,
        fc1_weight_grad,
        fc1_bias_grad,
        fc2_weight_grad,
    ) = lax.psum(
        (
            qkv_weight_grad,
            qv_bias_grad,
            dense_weight_grad,
            fc1_weight_grad,
            fc1_bias_grad,
            fc2_weight_grad,
        ),
        "dp",
    )
    (
        dense_bias_grad,
        norm1_gain_grad,
        norm1_shift_grad,
        norm2_gain_grad,
        norm2_shift_grad,
        fc2_bias_grad,
    ) = lax.psum(
        (
            dense_bias_grad,
            norm1_gain_grad,
            norm1_shift_grad,
            norm2_gain_grad,
            norm2_shift_grad,
            fc2_bias_grad,
        ),
        ("dp", "tensor"),
    )
    entry_count = rows_here * features * lax.axis_size("dp") * lax.axis_size("tensor")
    sublayer_rms = jnp.sqrt(totals_sq / float(entry_count))
    return (
        final.astype(jnp.bfloat16),
        hidden_grad,
        qkv_weight_grad,
        qv_bias_grad,
        dense_weight_grad,
        dense_bias_grad,
        norm1_gain_grad,
        norm1_shift_grad,
        norm2_gain_grad,
        norm2_shift_grad,
        fc1_weight_grad,
        fc1_bias_grad,
        fc2_weight_grad,
        fc2_bias_grad,
        sublayer_rms,
    )


def solution(mesh):
    return jax.shard_map(
        local,
        mesh=mesh,
        in_specs=(
            P(("dp", "tensor"), None),
            P(("dp", "tensor"), None),
            P("dp"),
            P(None, "tensor"),
            P("tensor", None, None),
            P("tensor", None),
            P(),
            P(),
            P(),
            P(),
            P(),
            P(None, "tensor"),
            P("tensor"),
            P("tensor", None),
            P(),
        ),
        out_specs=(
            P(("dp", "tensor"), None),
            P(("dp", "tensor"), None),
            P(None, "tensor"),
            P("tensor", None, None),
            P("tensor", None),
            P(),
            P(),
            P(),
            P(),
            P(),
            P(None, "tensor"),
            P("tensor"),
            P("tensor", None),
            P(),
            P(),
        ),
        check_vma=False,
    )
```

profile of v0, /device:TPU:0, one launch (start us, length us, event | category | flops | bytes accessed | tf_op | source)
XLA Modules:
  0.0 816.9 jit_solution(5367681616987311874)
XLA Ops:
  13.2 24.4 %all-gather.5.cloned.1.call-done = bf16[1024,1024]{1,0:T(8,128)(2,1)} async-done(((bf16[256,1024]{1,0:T(8,128)(2,1)}), bf16[1024,1024]{1,0:T(8,128)(2,1)}) %all-gather.5.cloned.1.call-update) | async-done | bytes 2097168 | tf_op jit(solution)/shard_map/all_gather | solution.py:157
  37.5 3.9 add_convert_fusion
  42.4 35.2 %while.28 = (s32[]{:T(128)}, bf16[2,512,4,64]{1,3,2,0:T(8,128)(2,1)}, f32[2,4,512]{2,1,0:T(4,128)S(1)}, s32[2]{0:T(128)S(1)}, s32[]{:T(128)}, /*index=5*/bf16[10...) while((s32[]{:T(128)}, ...), condition=%wide.region_5.6_spmd.clone, body=%wide.region_2.5_spmd.clone.sunk | while | flops 577896960 | bytes 41494816 | solution.py:74
  48.5 3.3 fusion.126
  54.8 4.4 fusion.128
  66.1 3.3 fusion.126
  72.4 4.4 fusion.128
  80.4 3.8 fusion.68
  84.4 44.4 %reduce-scatter.5.cloned.1.call-done = f32[256,1024]{1,0:T(8,128)} async-done(((f32[1024,1024]{1,0:T(8,128)}), f32[256,1024]{1,0:T(8,128)}) %reduce-scatter.5.cloned.1.call-update) | async-done | bytes 1048592 | tf_op jit(solution)/shard_map/reduce_scatter | solution.py:168
  133.7 22.1 %all-gather.7.cloned.1.call-done = bf16[1024,1024]{1,0:T(8,128)(2,1)} async-done(((bf16[256,1024]{1,0:T(8,128)(2,1)}), bf16[1024,1024]{1,0:T(8,128)(2,1)}) %all-gather.7.cloned.1.call-update) | async-done | bytes 2097168 | tf_op jit(solution)/shard_map/all_gather | solution.py:178
  155.8 4.6 fusion.69
  162.4 4.1 convolution_convert_fusion
  166.6 13.3 %all-gather.9.cloned.1.call-done = bf16[1024,1024]{1,0:T(8,128)(2,1)} async-done(((bf16[256,1024]{1,0:T(8,128)(2,1)}), bf16[1024,1024]{1,0:T(8,128)(2,1)}) %all-gather.9.cloned.1.call-update) | async-done | bytes 2097168 | tf_op jit(solution)/shard_map/all_gather | solution.py:200
  179.9 7.5 convert_reduce_fusion
  188.7 4.4 fusion.70
  193.2 21.3 %reduce-scatter.7.cloned.1.call-done = bf16[256,1024]{1,0:T(8,128)(2,1)} async-done(((bf16[1024,1024]{1,0:T(8,128)(2,1)}), bf16[256,1024]{1,0:T(8,128)(2,1)}) %reduce-scatter.7.cloned.1.call-update) | async-done | bytes 524304 | tf_op jit(solution)/shard_map/reduce_scatter | solution.py:182
  214.5 47.5 %reduce-scatter.9.cloned.1.call-done = f32[256,1024]{1,0:T(8,128)} async-done(((f32[1024,1024]{1,0:T(8,128)}), f32[256,1024]{1,0:T(8,128)}) %reduce-scatter.9.cloned.1.call-update) | async-done | bytes 1048592 | tf_op jit(solution)/shard_map/reduce_scatter | solution.py:207
  262.0 3.4 multiply_reduce_fusion.4
  269.5 22.7 %all-gather.11.cloned.1.call-done = bf16[1024,1024]{1,0:T(8,128)(2,1)} async-done(((bf16[256,1024]{1,0:T(8,128)(2,1)}), bf16[1024,1024]{1,0:T(8,128)(2,1)}) %all-gather.11.cloned.1.call-update) | async-done | bytes 2097168 | tf_op jit(solution)/shard_map/all_gather | solution.py:217
  295.4 57.1 %while.29 = (s32[]{:T(128)}, f32[1024,4,64]{0,2,1:T(8,128)S(1)}, f32[1024,4,64]{0,2,1:T(8,128)}, bf16[2,512,4,64]{1,0,3,2:T(2,128)(2,1)}, s32[2]{0:T(128)S(1)}, ...) while((s32[]{:T(128)}, f32[1024,4,64]{0,2,1:T(8,128)S(1)}, ...), condition=%wide.region_15.16_spmd.clone, body=%wide.region_13.15_spmd.clone.sunk | while | flops 1369965056 | bytes 84723520 | solution.py:121
  304.3 3.9 multiply_reduce_fusion.8
  314.3 9.8 %dynamic_update_slice.22 = bf16[2,512,4,64]{1,0,3,2:T(2,128)(2,1)} dynamic-update-slice(bf16[2,512,4,64]{1,0,3,2:T(2,128)(2,1)} %get-tuple-element.471, bf16[1,512,4,64]{1,0,3,2:T(2,128)(2,1)S(1)} %copy.67, s32[]{:T(128)S(6)} %copy.84, s32[]{:T(128)} %constant.48.clone.1..sunk.1, s32[]{:T(128)} %constant.48.clone.1..sunk.1, s32[]{:T(128)} %constant.48.clone.1..sunk.1) | dynamic-update-slice | bytes 524292 | tf_op jit(solution)/shard_map/while/body/jit(dynamic_update_index_in_dim)/dynamic_update_slice | solution.py:121
  332.7 3.9 multiply_reduce_fusion.8
  342.7 9.8 %dynamic_update_slice.22 = bf16[2,512,4,64]{1,0,3,2:T(2,128)(2,1)} dynamic-update-slice(bf16[2,512,4,64]{1,0,3,2:T(2,128)(2,1)} %get-tuple-element.471, bf16[1,512,4,64]{1,0,3,2:T(2,128)(2,1)S(1)} %copy.67, s32[]{:T(128)S(6)} %copy.84, s32[]{:T(128)} %constant.48.clone.1..sunk.1, s32[]{:T(128)} %constant.48.clone.1..sunk.1, s32[]{:T(128)} %constant.48.clone.1..sunk.1) | dynamic-update-slice | bytes 524292 | tf_op jit(solution)/shard_map/while/body/jit(dynamic_update_index_in_dim)/dynamic_update_slice | solution.py:121
  356.9 3.3 convolution_convert_fusion.1
  360.5 6.8 fusion.73
  367.3 5.1 fusion.63
  374.1 3.5 fusion.71
  377.9 22.3 %all-reduce.1 = (f32[4,2,64]{2,1,0:T(2,128)}, f32[1024]{0:T(1024)}) all-reduce(f32[4,2,64]{2,1,0:T(2,128)S(1)} %pad_maximum_fusion.1, f32[1024]{0:T(1024)S(1)} %get-tuple-element.262), channel_id=1, replica_groups=mesh['dp'=8,'tensor'=4] {'dp'}, use_global_device_ids=true, to_apply=%region_22.23 | all-reduce | flops 1536 | bytes 12288 | tf_op jit(solution)/shard_map/psum | solution.py:249
  409.4 42.4 %all-reduce = (f32[1024]{0:T(1024)}, f32[1024]{0:T(1024)}, f32[1024]{0:T(1024)}, f32[1024]{0:T(1024)}, f32[1024]{0:T(1024)}, /*index=5*/f32[1024]{0:T(1024)}, f32[4]{0:T(128)S(1)}) all-reduce(f32[1024]{0:T(1024)S(1)} %get-tuple-element.206, f32[1024]{0:T(1024)S(1)} %get-tuple-element.199, ...), channel_id=1, replica_groups=mesh['dp'=8,'tensor'=4] {'dp','tensor'}, use_global_device_ids=true, to_apply=%region_25.26 | all-reduce | flops 6148 | bytes 49184 | tf_op jit(solution)/shard_map/psum | solution.py:267
  452.3 347.0 %all-reduce.5.cloned.1.call-done = (f32[1024,768]{1,0:T(8,128)}, f32[256,1024]{1,0:T(8,128)}, f32[1024,1024]{1,0:T(8,128)}, f32[1024,1024]{1,0:T(8,128)}) async-done(((f32[1024,768]{1,0:T(8,128)}, f32[256,1024]{1,0:T(8,128)}, f32[1024,1024]{1,0:T(8,128)}, f32[1024,1024]{1,0:T(8,128)}), (f32[1024,768]{1,0:T(8,128)}, f32[256,1024]{1,0:T(8,128)}, f32[1024,1024]{1,0:T(8,128)}, ...) | async-done | bytes 12582928 | tf_op jit(solution)/shard_map/psum | solution.py:249
  799.3 3.9 copy.96
  (199 shorter events, 89.5 us)
Async XLA Ops:
  7.2 155.2 %copy-start = (bf16[1024,1024]{1,0:T(8,128)(2,1)S(1)}, bf16[1024,1024]{1,0:T(8,128)(2,1)}, u32[]{:S(2)}) copy-start(bf16[1024,1024]{1,0:T(8,128)(2,1)} %param.32) | copy-start | bytes 6291460
  7.2 30.3 %all-gather.5.cloned.1.call-start = ((), (), s32[]{:S(2)}) async-start(), calls=%async_computation.4 | async-start | bytes 2621440 | tf_op jit(solution)/shard_map/all_gather | solution.py:157
  8.6 32.9 %copy-start.24 = (f32[256]{0:T(256)}, f32[256]{0:T(256)S(1)}, u32[]{:S(2)}) copy-start(f32[256]{0:T(256)S(1)} %broadcast_multiply_fusion.1) | copy-start | bytes 3076
  12.1 116.7 %reduce-scatter.5.cloned.1.call-start = ((), (), s32[]{:S(2)}) async-start(), calls=%async_computation.5 | async-start | bytes 5242880 | tf_op jit(solution)/shard_map/reduce_scatter | solution.py:168
  84.2 44.7 %copy-start.6 = (bf16[256,1024]{1,0:T(8,128)(2,1)S(1)}, bf16[256,1024]{1,0:T(8,128)(2,1)}, u32[]{:S(2)}) copy-start(bf16[256,1024]{1,0:T(8,128)(2,1)} %param.19) | copy-start | bytes 1572868
  84.2 44.7 %copy-start.30 = (f32[1024]{0:T(1024)S(1)}, f32[1024]{0:T(1024)}, u32[]{:S(2)}) copy-start(f32[1024]{0:T(1024)} %param.25) | copy-start | bytes 12292
  84.2 47.8 %copy-start.23 = (f32[1024]{0:T(1024)S(1)}, f32[1024]{0:T(1024)}, u32[]{:S(2)}) copy-start(f32[1024]{0:T(1024)} %param.28) | copy-start | bytes 12292
  84.2 47.8 %copy-start.31 = (f32[1024]{0:T(1024)S(1)}, f32[1024]{0:T(1024)}, u32[]{:S(2)}) copy-start(f32[1024]{0:T(1024)} %param.29) | copy-start | bytes 12292
  84.2 71.6 %all-gather.7.cloned.1.call-start = ((), (), s32[]{:S(2)}) async-start(), calls=%async_computation.6 | async-start | bytes 2621440 | tf_op jit(solution)/shard_map/all_gather | solution.py:178
  133.0 46.9 %all-gather.9.cloned.1.call-start = ((), (), s32[]{:S(2)}) async-start(), calls=%async_computation.8 | async-start | bytes 2621440 | tf_op jit(solution)/shard_map/all_gather | solution.py:200
  133.6 28.7 %copy-start.37 = (f32[1024]{0:T(1024)S(1)}, f32[1024]{0:T(1024)}, u32[]{:S(2)}) copy-start(f32[1024]{0:T(1024)} %param.31) | copy-start | bytes 12292
  133.6 80.8 %reduce-scatter.7.cloned.1.call-start = ((), (), s32[]{:S(2)}) async-start(), calls=%async_computation.7 | async-start | bytes 2621440 | tf_op jit(solution)/shard_map/reduce_scatter | solution.py:182
  166.5 95.4 %reduce-scatter.9.cloned.1.call-start = ((), (), s32[]{:S(2)}) async-start(), calls=%async_computation.9 | async-start | bytes 5242880 | tf_op jit(solution)/shard_map/reduce_scatter | solution.py:207
  179.9 8.8 %copy-start.33 = (bf16[1024,1024]{1,0:T(8,128)(2,1)S(1)}, bf16[1024,1024]{1,0:T(8,128)(2,1)}, u32[]{:S(2)}) copy-start(bf16[1024,1024]{1,0:T(8,128)(2,1)} %param.30) | copy-start | bytes 6291460
  193.1 68.9 %copy-start.5 = (f32[256,1024]{1,0:T(8,128)S(1)}, f32[256,1024]{1,0:T(8,128)}, u32[]{:S(2)}) copy-start(f32[256,1024]{1,0:T(8,128)} %copy-done.4) | copy-start | bytes 3145732
  193.1 68.9 %copy-start.32 = (f32[1024]{0:T(1024)S(1)}, f32[1024]{0:T(1024)}, u32[]{:S(2)}) copy-start(f32[1024]{0:T(1024)} %param.33) | copy-start | bytes 12292
  193.1 99.1 %all-gather.11.cloned.1.call-start = ((), (), s32[]{:S(2)}) async-start(), calls=%async_computation.10 | async-start | bytes 2621440 | tf_op jit(solution)/shard_map/all_gather | solution.py:217
  267.0 28.4 %copy-start.10 = (f32[256,1024]{1,0:T(8,128)}, f32[256,1024]{1,0:T(8,128)S(1)}, u32[]{:S(2)}) copy-start(f32[256,1024]{1,0:T(8,128)S(1)} %get-tuple-element.265) | copy-start | bytes 3145732
  267.0 28.4 %copy-start.9 = (bf16[1024,4,64]{0,2,1:T(8,128)(2,1)S(1)}, bf16[1024,4,64]{0,2,1:T(8,128)(2,1)}, u32[]{:S(2)}) copy-start(bf16[1024,4,64]{0,2,1:T(8,128)(2,1)} %copy-done.8) | copy-start | bytes 1572868
  269.5 130.8 %reduce-scatter.11.cloned.1.call-start = ((), (), s32[]{:S(2)}) async-start(), calls=%async_computation.11 | async-start | bytes 2621440 | tf_op jit(solution)/shard_map/reduce_scatter | solution.py:232
  360.2 439.1 %all-reduce.5.cloned.1.call-start = ((), (), s32[]{:S(2)}) async-start(), calls=%async_computation.12 | async-start | bytes 25165824 | tf_op jit(solution)/shard_map/psum | solution.py:249
  360.5 6.8 copy-start.35
  360.5 6.8 copy-start.39
  367.3 6.8 copy-start.18
  367.3 6.8 copy-start.34
  377.6 22.6 %copy-start.7 = (bf16[256,1024]{1,0:T(8,128)(2,1)S(1)}, bf16[256,1024]{1,0:T(8,128)(2,1)}, u32[]{:S(2)}) copy-start(bf16[256,1024]{1,0:T(8,128)(2,1)} %param.19) | copy-start | bytes 1572868
  377.6 22.6 %copy-start.22 = (f32[1024]{0:T(1024)S(1)}, f32[1024]{0:T(1024)}, u32[]{:S(2)}) copy-start(f32[1024]{0:T(1024)} %param.26) | copy-start | bytes 12292
  377.6 22.6 %copy-start.25 = (f32[256]{0:T(256)S(1)}, f32[256]{0:T(256)}, u32[]{:S(2)}) copy-start(f32[256]{0:T(256)} %copy-done.24) | copy-start | bytes 3076
  377.6 24.0 %copy-start.29 = (f32[256]{0:T(256)S(1)}, f32[256]{0:T(256)}, u32[]{:S(2)}) copy-start(f32[256]{0:T(256)} %copy-done.28) | copy-start | bytes 3076
  377.6 24.0 %copy-start.27 = (f32[256]{0:T(256)S(1)}, f32[256]{0:T(256)}, u32[]{:S(2)}) copy-start(f32[256]{0:T(256)} %copy-done.26) | copy-start | bytes 3076
  377.7 29.0 %copy-start.13 = (bf16[256,1024]{1,0:T(8,128)(2,1)S(1)}, bf16[256,1024]{1,0:T(8,128)(2,1)}, u32[]{:S(2)}) copy-start(bf16[256,1024]{1,0:T(8,128)(2,1)} %param.20) | copy-start | bytes 1572868
  804.2 5.7 copy-start.1
  (22 other events, 52.8 us)
Sparse Core Ops, SparseCore 0:
  12.2 25.2 all-gather.4
  84.3 44.4 reduce-scatter.4
  133.2 22.5 all-gather.6
  157.3 22.5 all-gather.8
  183.0 31.4 reduce-scatter.6
  217.4 44.4 reduce-scatter.8
  269.6 22.5 all-gather.10
  360.3 31.4 reduce-scatter.10
  397.7 401.5 all-reduce.4
where the time goes:
time: 828 us; the launch traced here: 817 us
  waiting for transfers between devices  543 us (66%)
  matrix products  89 us (11%)
  blocking collectives  64.7 us (8%)
  other arithmetic  49.1 us (6%)
  local copies, waits for them, and re-layouts  46.9 us (6%)
  between operations  14.7 us (2%)
  loops' own time  8.35 us (1%)
    psum x1, waiting for transfers between devices, local(): lax.psum((qkv_weight_grad, qv_bias_grad, dense_weight_grad, fc1_weight_gr...  347 us
    reduce_scatter x1, waiting for transfers between devices, local(): lax.psum_scatter(contract_cols(pre_grad, fc1_weight), 'tensor', scatter_d...  47.5 us
    reduce_scatter x1, waiting for transfers between devices, local(): lax.psum_scatter(jnp.dot(context, dense_weight, preferred_element_type=jn...  44.4 us
    psum x1, blocking collectives, local(): lax.psum((dense_bias_grad, norm1_gain_grad, norm1_shift_grad, norm2_gain_...  42.4 us
    all_gather x1, waiting for transfers between devices, local(): normed1_all = lax.all_gather(normed1, 'tensor', axis=0, tiled=True)  24.4 us
    all_gather x1, waiting for transfers between devices, local(): lax.all_gather(middle_grad.astype(jnp.bfloat16), 'tensor', axis=0, tiled=...  22.7 us
    psum x1, blocking collectives, local(): lax.psum((qkv_weight_grad, qv_bias_grad, dense_weight_grad, fc1_weight_gr...  22.3 us
    all_gather x1, waiting for transfers between devices, local(): normed2_all = lax.all_gather(normed2, 'tensor', axis=0, tiled=True)  22.1 us
  transfers between devices with their start and end apart: 9, of which 8 were waited for; matrix products, arithmetic and copies ran while one was open for 6% of the time, Pallas kernels for 0%

commit v1 on v0

v1 whole, which is shorter than its diff:
```python
from functools import partial

import jax
import jax.numpy as jnp
from jax import lax
from jax.experimental import pallas as pl
from jax.experimental.pallas import tpu as pltpu
from jax.sharding import PartitionSpec as P

HEADS = 16
PREFIX_MOST = 512

epsilon = 1e-05
BF = jnp.bfloat16
F32 = jnp.float32
NT = (((1,), (1,)), ((), ()))
NN = (((1,), (0,)), ((), ()))
TN = (((0,), (0,)), ((), ()))


def dot(a, b, dims):
    return lax.dot_general(a, b, dims, preferred_element_type=F32)


def after(value, *others):
    return lax.optimization_barrier((value,) + others)[0]


def norm_parts(values):
    center = jnp.mean(values, axis=-1, keepdims=True)
    deviation = values - center
    variance = jnp.mean(deviation * deviation, axis=-1, keepdims=True)
    rstd = lax.rsqrt(variance + epsilon)
    return deviation * rstd, rstd


def norm_backward(values, gain, upstream):
    unit, rstd = norm_parts(values)
    scaled = upstream * gain
    grad = rstd * (
        scaled
        - jnp.mean(scaled, axis=-1, keepdims=True)
        - unit * jnp.mean(scaled * unit, axis=-1, keepdims=True)
    )
    return grad, jnp.sum(upstream * unit, axis=0), jnp.sum(upstream, axis=0)


def split3(value):
    high = value.astype(BF).astype(F32)
    rest = value - high
    mid = rest.astype(BF).astype(F32)
    return high, mid, rest - mid


def place(lane, base, items):
    out = jnp.zeros(lane.shape, F32)
    for i, item in enumerate(items):
        out = jnp.where(lane == base + i, item, out)
    return out


def causal_end(row_block, size, length):
    return min(max((row_block + 1) * size, min(PREFIX_MOST, length)), length)


def fill_masks(masks, prefix, size, blocks, transposed):
    shape = (size, size)
    for index, (row_block, col_block) in enumerate(blocks):
        rows = row_block * size + lax.broadcasted_iota(jnp.int32, shape, 1 if transposed else 0)
        cols = col_block * size + lax.broadcasted_iota(jnp.int32, shape, 0 if transposed else 1)
        allowed = (cols <= rows) | ((cols < prefix) & (rows < prefix))
        beyond = jnp.maximum(cols - rows, 0).astype(F32)
        masks[index] = jnp.where(allowed, -2.0 * beyond, -1e30)


def special_blocks(length, size):
    out = []
    for row_block in range(length // size):
        for col_block in range(causal_end(row_block, size, length) // size):
            if col_block >= row_block:
                out.append((row_block, col_block))
    return out


def attend_forward_kernel(size, prefix_ref, slope_ref, joined_ref, context_ref, total_ref, masks):
    length = joined_ref.shape[0]
    pair = pl.program_id(0)
    blocks = special_blocks(length, size)

    @pl.when(pair == 0)
    def _():
        fill_masks(masks, prefix_ref[0], size, blocks, False)

    lane = lax.broadcasted_iota(jnp.int32, (length, 128), 1)
    low = lane < 64
    position = lax.broadcasted_iota(jnp.int32, (length, 1), 0).astype(F32)
    tiles = [joined_ref[:, i * 128 : (i + 1) * 128].astype(F32) for i in range(3)]
    rolled0 = pltpu.roll(tiles[0], 64, 1)
    rolled1 = pltpu.roll(tiles[1], 64, 1)
    sides = []
    for head in range(2):
        slope = slope_ref[pair * 2 + head]
        own = jnp.logical_not(low) if head == 0 else low
        base = 0 if head == 0 else 64
        query = jnp.where(own, (rolled0 if head == 0 else rolled1) * 0.125, place(lane, base, (1.0, 1.0, 1.0)))
        keys = jnp.where(own, tiles[0] if head == 0 else tiles[2], place(lane, base, split3(slope * position)))
        value = jnp.where(low, tiles[1], 1.0) if head == 0 else jnp.where(low, 1.0, tiles[2])
        sides.append((slope, query.astype(BF), keys.astype(BF), value.astype(BF)))
    low_block = low[:size]
    lane_block = lane[:size]
    for row_block in range(length // size):
        end = causal_end(row_block, size, length)
        rows = slice(row_block * size, (row_block + 1) * size)
        results = []
        for head in range(2):
            slope, query, keys, value = sides[head]
            scores = dot(query[rows], keys[:end], NT)
            columns = []
            for col_block in range(end // size):
                piece = scores[:, col_block * size : (col_block + 1) * size]
                if col_block >= row_block:
                    piece = piece + slope * masks[blocks.index((row_block, col_block))]
                columns.append(piece)
            highest = columns[0]
            for piece in columns[1:]:
                highest = jnp.maximum(highest, piece)
            highest = jnp.max(highest, axis=-1, keepdims=True)
            powered = jnp.concatenate([jnp.exp(piece - highest).astype(BF) for piece in columns], axis=1)
            gathered = dot(powered, value[:end], NN)
            total = gathered[:, 64:65] if head == 0 else gathered[:, 0:1]
            results.append((gathered / total, highest + jnp.log(total)))
        context_ref[rows, :] = jnp.where(low_block, results[0][0], results[1][0]).astype(BF)
        total_ref[rows, :] = jnp.where(lane_block == 0, results[0][1], results[1][1])


def attend_forward(joined, prefix, slopes, size=256):
    length, columns = joined.shape
    pairs = columns // 384
    count = len(special_blocks(length, size))
    return pl.pallas_call(
        partial(attend_forward_kernel, size),
        grid_spec=pltpu.PrefetchScalarGridSpec(
            num_scalar_prefetch=2,
            grid=(pairs,),
            in_specs=[pl.BlockSpec((length, 384), lambda p, *_: (0, p))],
            out_specs=[
                pl.BlockSpec((length, 128), lambda p, *_: (0, p)),
                pl.BlockSpec((length, 128), lambda p, *_: (0, p)),
            ],
            scratch_shapes=[pltpu.VMEM((count, size, size), F32)],
        ),
        out_shape=[
            jax.ShapeDtypeStruct((length, pairs * 128), BF),
            jax.ShapeDtypeStruct((length, pairs * 128), F32),
        ],
        compiler_params=pltpu.CompilerParams(vmem_limit_bytes=40 * 1024 * 1024),
        cost_estimate=pl.CostEstimate(flops=pairs * 2 * 2 * 2 * length * length * 128, bytes_accessed=4 * 1024 * 1024, transcendentals=0),
        name="attend_forward",
    )(prefix, slopes, joined)


def attend_backward_kernel(size, prefix_ref, slope_ref, joined_ref, total_ref, context_ref, grad_ref, out_ref, masks, query_sum):
    length = joined_ref.shape[0]
    pair = pl.program_id(0)
    blocks = special_blocks(length, size)

    @pl.when(pair == 0)
    def _():
        fill_masks(masks, prefix_ref[0], size, blocks, True)

    lane = lax.broadcasted_iota(jnp.int32, (length, 128), 1)
    low = lane < 64
    position = lax.broadcasted_iota(jnp.int32, (length, 1), 0).astype(F32)
    tiles = [joined_ref[:, i * 128 : (i + 1) * 128].astype(F32) for i in range(3)]
    rolled = [pltpu.roll(tile, 64, 1) for tile in tiles]
    grad = grad_ref[...].astype(F32)
    product = grad * context_ref[...].astype(F32)
    grad_low = grad.astype(BF)
    rolled_low = [tile.astype(BF) for tile in rolled]
    sides = []
    for head in range(2):
        slope = slope_ref[pair * 2 + head]
        own = jnp.logical_not(low) if head == 0 else low
        base = 0 if head == 0 else 64
        log_total = total_ref[:, head : head + 1]
        query = jnp.where(
            own, rolled[head] * 0.125, place(lane, base, (1.0, 1.0, 1.0) + split3(log_total))
        )
        keys = jnp.where(
            own, tiles[0] if head == 0 else tiles[2], place(lane, base, split3(slope * position) + (-1.0, -1.0, -1.0))
        )
        head_lanes = low if head == 0 else jnp.logical_not(low)
        inner = jnp.sum(jnp.where(head_lanes, product, 0.0), axis=1, keepdims=True)
        base = 64 - base
        value = jnp.where(head_lanes, tiles[1] if head == 0 else tiles[2], place(lane, 64 if head == 0 else 0, (-1.0, -1.0, -1.0)))
        upstream = jnp.where(head_lanes, grad, place(lane, 64 if head == 0 else 0, split3(inner)))
        sides.append((slope, query.astype(BF), keys.astype(BF), value.astype(BF), upstream.astype(BF)))
    low_block = low[:size]
    for col_block in range(length // size):
        first = col_block if col_block * size >= PREFIX_MOST else 0
        cols = slice(col_block * size, (col_block + 1) * size)
        start = first * size
        results = []
        for head in range(2):
            slope, query, keys, value, upstream = sides[head]
            scores = dot(keys[cols], query[start:], NT)
            prob_grad = dot(value[cols], upstream[start:], NT)
            weights, score_grads = [], []
            for row_block in range(first, length // size):
                at = slice((row_block - first) * size, (row_block - first + 1) * size)
                piece = scores[:, at]
                if col_block >= row_block:
                    piece = piece + slope * masks[blocks.index((row_block, col_block))]
                powered = jnp.exp(piece)
                weights.append(powered.astype(BF))
                score_grads.append((powered * prob_grad[:, at]).astype(BF))
            weights = jnp.concatenate(weights, axis=1)
            score_grads = jnp.concatenate(score_grads, axis=1)
            value_grad = dot(weights, grad_low[start:], NN)
            key_grad = dot(score_grads, rolled_low[head][start:], NN) * 0.125
            query_grad = dot(score_grads, rolled_low[0 if head == 0 else 2][cols], TN)
            if col_block == 0:
                query_sum[head] = query_grad
            else:
                query_sum[head, start:] = query_sum[head, start:] + query_grad
            results.append((key_grad, value_grad))
        (key0, value0), (key1, value1) = results
        out_ref[cols, 0:128] = key0.astype(BF)
        out_ref[cols, 128:256] = value0.astype(BF)
        out_ref[cols, 256:384] = jnp.where(low_block, key1, value1).astype(BF)
    out_ref[:, 0:128] = jnp.where(low, query_sum[0] * 0.125, out_ref[:, 0:128].astype(F32)).astype(BF)
    out_ref[:, 128:256] = jnp.where(low, out_ref[:, 128:256].astype(F32), query_sum[1] * 0.125).astype(BF)


def attend_backward(joined, log_totals, context, context_grad, prefix, slopes, size=256):
    length, columns = joined.shape
    pairs = columns // 384
    count = len(special_blocks(length, size))
    return pl.pallas_call(
        partial(attend_backward_kernel, size),
        grid_spec=pltpu.PrefetchScalarGridSpec(
            num_scalar_prefetch=2,
            grid=(pairs,),
            in_specs=[
                pl.BlockSpec((length, 384), lambda p, *_: (0, p)),
                pl.BlockSpec((length, 128), lambda p, *_: (0, p)),
                pl.BlockSpec((length, 128), lambda p, *_: (0, p)),
                pl.BlockSpec((length, 128), lambda p, *_: (0, p)),
            ],
            out_specs=pl.BlockSpec((length, 384), lambda p, *_: (0, p)),
            scratch_shapes=[pltpu.VMEM((count, size, size), F32), pltpu.VMEM((2, length, 128), F32)],
        ),
        out_shape=jax.ShapeDtypeStruct((length, columns), BF),
        compiler_params=pltpu.CompilerParams(vmem_limit_bytes=48 * 1024 * 1024),
        cost_estimate=pl.CostEstimate(flops=pairs * 2 * 5 * 2 * length * length * 128, bytes_accessed=6 * 1024 * 1024, transcendentals=0),
        name="attend_backward",
    )(prefix, slopes, joined, log_totals, context, context_grad)


def tensor_send(value, flip):
    return lax.ppermute(value, "tensor", [(i, i ^ flip) for i in range(4)])


def gather_blocks(value, gate=()):
    if gate:
        value = after(value, *gate)
    over_core = tensor_send(value, 1)
    over_x = tensor_send(value, 2)
    return [value, over_core, over_x, tensor_send(over_x, 1)]


def in_order(blocks, me):
    rows = blocks[0].shape[0]
    out = jnp.zeros((4 * rows, blocks[0].shape[1]), blocks[0].dtype)
    for flip, block in enumerate(blocks):
        out = lax.dynamic_update_slice_in_dim(out, block, (me ^ flip) * rows, 0)
    return out


def scatter_sum(block_of):
    over = tensor_send(block_of(3).astype(BF), 1)
    chip = (block_of(2) + over.astype(F32)).astype(BF)
    far = tensor_send(chip, 2)
    near = tensor_send(block_of(1).astype(BF), 1)
    return block_of(0) + near.astype(F32) + far.astype(F32)


def add_low(a, b):
    return (a.astype(F32) + b.astype(F32)).astype(BF)


def chain_sum(value, count, inner, place_of):
    def send(v, pairs):
        return lax.ppermute(v, "dp", [(a * inner + i, b * inner + i) for a, b in pairs for i in range(inner)])

    if count == 1:
        return value
    half = count // 2
    for step in range(half - 1):
        value = add_low(value, send(value, [(step, step + 1), (count - 1 - step, count - 2 - step)]))
    value = add_low(value, send(value, [(half - 1, half), (half, half - 1)]))
    for step in reversed(range(half - 1)):
        came = send(value, [(step + 1, step), (count - 2 - step, count - 1 - step)])
        value = jnp.where((place_of <= step) | (place_of >= count - 1 - step), came, value)
    return value


def dp_sum(term_of, rows, chunks, dp):
    inner = 2
    outer = dp // inner
    index = lax.axis_index("dp")
    mine, place_of = index % inner, index // inner
    pairs = [(i, i ^ 1) for i in range(dp)]
    size = rows // chunks
    half = size // 2
    pieces = []
    for chunk in range(chunks):
        sent = term_of(chunk * size + (1 - mine) * half, half).astype(BF)
        came = lax.ppermute(sent, "dp", pairs)
        value = (term_of(chunk * size + mine * half, half) + came.astype(F32)).astype(BF)
        value = chain_sum(value, outer, inner, place_of)
        other = lax.ppermute(value, "dp", pairs)
        first = jnp.where(mine == 0, value, other)
        second = jnp.where(mine == 0, other, value)
        pieces += [first, second]
    return jnp.concatenate(pieces, axis=0).astype(F32)


def small_sum(value, dp, axes):
    if "dp" in axes:
        step = 1
        while step < dp:
            value = value + lax.ppermute(value, "dp", [(i, i ^ step) for i in range(dp)])
            step *= 2
    if "tensor" in axes:
        for step in (1, 2):
            value = value + tensor_send(value, step)
    return value


def local(
    dp,
    hidden_in,
    out_grad,
    prefix_len,
    qkv_weight,
    qv_bias,
    dense_weight,
    dense_bias,
    norm1_gain,
    norm1_shift,
    norm2_gain,
    norm2_shift,
    fc1_weight,
    fc1_bias,
    fc2_weight,
    fc2_bias,
):
    rows_here, features = hidden_in.shape
    heads_here, _, head_size = qv_bias.shape
    me = lax.axis_index("tensor")
    slopes = 2.0 ** (-8.0 * (me * heads_here + 1 + lax.iota(jnp.int32, heads_here)).astype(F32) / HEADS)

    hidden_blocks = gather_blocks(hidden_in)
    dense_blocks = gather_blocks(dense_weight, (hidden_blocks[2],))
    grad_blocks = gather_blocks(out_grad, (dense_blocks[2],))

    residual_all = in_order(hidden_blocks, me).astype(F32)
    residual = hidden_in.astype(F32)
    length = residual_all.shape[0]
    normed1_all = (norm_parts(residual_all)[0] * norm1_gain + norm1_shift).astype(BF)
    bias_full = jnp.stack(
        [qv_bias[:, 0], jnp.zeros_like(qv_bias[:, 0]), qv_bias[:, 1]], axis=1
    ).reshape(-1)
    joined = (dot(normed1_all, qkv_weight, NN) + bias_full).astype(BF)
    context, log_totals = attend_forward(joined, prefix_len, slopes)
    context_blocks = gather_blocks(context)
    context_cat = jnp.concatenate(context_blocks, axis=1)
    dense_cat = jnp.concatenate(dense_blocks, axis=0)
    attn_all = dot(context_cat, dense_cat, NN) + dense_bias
    middle_all = residual_all + attn_all
    normed2_all = (norm_parts(middle_all)[0] * norm2_gain + norm2_shift).astype(BF)
    attn_out = lax.dynamic_slice_in_dim(attn_all, me * rows_here, rows_here, 0)
    middle = lax.dynamic_slice_in_dim(middle_all, me * rows_here, rows_here, 0)
    pre = dot(normed2_all, fc1_weight, NN) + fc1_bias
    cubic = 0.7978845608028654
    inner = jnp.tanh(cubic * (pre + 0.044715 * pre * pre * pre))
    activated = (0.5 * pre * (1.0 + inner)).astype(BF)
    slope_pre = 0.5 * (1.0 + inner) + 0.5 * pre * (1.0 - inner * inner) * cubic * (1.0 + 3 * 0.044715 * pre * pre)

    grad_all = in_order(grad_blocks, me)
    act_grad = dot(grad_all, fc2_weight, NT)
    pre_grad = (act_grad * slope_pre).astype(BF)

    def columns_of(array):
        return lambda first, count: lax.dynamic_slice_in_dim(array, first, count, 1)

    act_cols, pre_cols, normed2_cols = columns_of(activated), columns_of(pre_grad), columns_of(normed2_all)
    fc2_weight_grad = dp_sum(lambda a, n: dot(act_cols(a, n), grad_all, TN), activated.shape[1], 4, dp)
    fc1_weight_grad = dp_sum(lambda a, n: dot(normed2_cols(a, n), pre_grad, TN), features, 4, dp)

    def rows_of(array):
        return lambda flip: lax.dynamic_slice_in_dim(array, (me ^ flip) * rows_here, rows_here, 0)

    pre_rows, act_rows = rows_of(pre_grad), rows_of(activated)
    normed2_grad = scatter_sum(lambda flip: dot(pre_rows(flip), fc1_weight, NT))

    gout = out_grad.astype(F32)
    middle_norm_grad, norm2_gain_grad, norm2_shift_grad = norm_backward(middle, norm2_gain, normed2_grad)
    middle_grad = gout + middle_norm_grad
    middle_low = middle_grad.astype(BF)
    context_grads = [dot(middle_low, weight, NT).astype(BF) for weight in dense_blocks]
    arrived = [context_grads[0]] + [tensor_send(context_grads[flip], flip) for flip in (1, 2, 3)]
    context_grad = in_order(arrived, me)
    middle_all_low = in_order(gather_blocks(middle_low, (context_grad,)), me)
    context_cols = columns_of(context)
    dense_weight_grad = dp_sum(lambda a, n: dot(context_cols(a, n), middle_all_low, TN), context.shape[1], 1, dp)

    mlp_out = scatter_sum(lambda flip: dot(act_rows(flip), fc2_weight, NN)) + fc2_bias
    final = middle + mlp_out

    joined_grad = attend_backward(joined, log_totals, context, context_grad, prefix_len, slopes)
    normed1_cols = columns_of(normed1_all)
    qkv_weight_grad = dp_sum(lambda a, n: dot(normed1_cols(a, n), joined_grad, TN), features, 4, dp)
    joined_rows = rows_of(joined_grad)
    normed1_grad = scatter_sum(lambda flip: dot(joined_rows(flip), qkv_weight, NT))
    input_norm_grad, norm1_gain_grad, norm1_shift_grad = norm_backward(residual, norm1_gain, normed1_grad)
    hidden_grad = (middle_grad + input_norm_grad).astype(BF)

    joined_sums = jnp.sum(joined_grad.astype(F32), axis=0).reshape(heads_here, 3, head_size)
    qv_sums = jnp.stack([joined_sums[:, 0], joined_sums[:, 2]], axis=1).reshape(-1)
    squares = jnp.stack(
        [
            jnp.sum(residual * residual),
            jnp.sum(attn_out * attn_out),
            jnp.sum(mlp_out * mlp_out),
            jnp.sum(final * final),
        ]
    )
    by_dp = small_sum(
        jnp.stack(
            [
                jnp.sum(pre_grad.astype(F32), axis=0),
                jnp.pad(qv_sums, (0, features - qv_sums.shape[0])),
                jnp.pad(squares, (0, features - 4)),
                jnp.sum(middle_grad, axis=0),
                norm1_gain_grad,
                norm1_shift_grad,
                norm2_gain_grad,
                norm2_shift_grad,
                jnp.sum(gout, axis=0),
            ]
        ),
        dp,
        ("dp",),
    )
    by_all = small_sum(by_dp[2:], dp, ("tensor",))
    fc1_bias_grad = by_dp[0]
    qv_bias_grad = by_dp[1, : qv_sums.shape[0]].reshape(heads_here, 2, head_size)
    entry_count = rows_here * features * dp * 4
    sublayer_rms = jnp.sqrt(by_all[0, :4] / float(entry_count))
    return (
        final.astype(BF),
        hidden_grad,
        qkv_weight_grad,
        qv_bias_grad,
        dense_weight_grad,
        by_all[1],
        by_all[2],
        by_all[3],
        by_all[4],
        by_all[5],
        fc1_weight_grad,
        fc1_bias_grad,
        fc2_weight_grad,
        by_all[6],
        sublayer_rms,
    )


def solution(mesh):
    return jax.shard_map(
        partial(local, mesh.shape["dp"]),
        mesh=mesh,
        in_specs=(
            P(("dp", "tensor"), None),
            P(("dp", "tensor"), None),
            P("dp"),
            P(None, "tensor"),
            P("tensor", None, None),
            P("tensor", None),
            P(),
            P(),
            P(),
            P(),
            P(),
            P(None, "tensor"),
            P("tensor"),
            P("tensor", None),
            P(),
        ),
        out_specs=(
            P(("dp", "tensor"), None),
            P(("dp", "tensor"), None),
            P(None, "tensor"),
            P("tensor", None, None),
            P("tensor", None),
            P(),
            P(),
            P(),
            P(),
            P(),
            P(None, "tensor"),
            P("tensor"),
            P("tensor", None),
            P(),
            P(),
        ),
        check_vma=False,
    )
```

time: 828 us -> 508 us (0.61)
  waiting for transfers between devices: 543 us -> 220 us
  starting transfers between devices: 0.79 us -> 124 us
  blocking collectives: 64.7 us -> 0 us
  matrix products: 89 us -> 55.9 us
  Pallas kernels: 0 us -> 20.5 us
  local copies, waits for them, and re-layouts: 46.9 us -> 31 us
  between operations: 14.7 us -> 3.61 us
  loops' own time: 8.35 us -> 0 us
    psum x1 -> x0, waiting for transfers between devices: 347 us -> none  [local(): lax.psum((qkv_weight_grad, qv_bias_grad, dense_weight_grad, fc1_weight_gr...]
    ppermute x0 -> x97, waiting for transfers between devices: none -> 220 us  [the longest x39 122 us: send(): lax.ppermute(v, 'dp', [(a * inner + i, b * inner + i) for a, b in pairs f...]
    ppermute x0 -> x97, starting transfers between devices: none -> 124 us  [the longest x39 75.5 us: send(): lax.ppermute(v, 'dp', [(a * inner + i, b * inner + i) for a, b in pairs f...]
    reduce_scatter x4 -> x0, waiting for transfers between devices: 113 us -> none  [the longest x1 47.5 us: local(): lax.psum_scatter(contract_cols(pre_grad, fc1_weight), 'tensor', scatter_d...]
    all_gather x4 -> x0, waiting for transfers between devices: 82.5 us -> none  [the longest x1 24.4 us: local(): normed1_all = lax.all_gather(normed1, 'tensor', axis=0, tiled=True)]
    psum x2 -> x0, blocking collectives: 64.7 us -> none  [the longest x1 42.4 us: local(): lax.psum((dense_bias_grad, norm1_gain_grad, norm1_shift_grad, norm2_gain_...]
    dot_general x26 -> x46, matrix products: 89 us -> 55.9 us  [dot(): return lax.dot_general(a, b, dims, preferred_element_type=F32)]
    pallas_call x0 -> x2, Pallas kernels: none -> 20.5 us  [the longest x1 12 us: attend_backward(): pl.pallas_call(partial(attend_backward_kernel, size), grid_spec=pltpu.Pre...]
  transfers between devices with their start and end apart: 9 -> 97, of which waited for: 8 -> 46; matrix products, arithmetic and copies ran while one was open for 6% -> 21% of each run, Pallas kernels for 0% -> 4%
where the time goes in v1:
time: 508 us; the launch traced here: 499 us
  waiting for transfers between devices  220 us (43%)
  starting transfers between devices  124 us (24%)
  matrix products  55.9 us (11%)
  other arithmetic  43.3 us (9%)
  local copies, waits for them, and re-layouts  31 us (6%)
  Pallas kernels  20.5 us (4%)
    ppermute x39, waiting for transfers between devices, send(): lax.ppermute(v, 'dp', [(a * inner + i, b * inner + i) for a, b in pairs f...  122 us
    ppermute x39, starting transfers between devices, send(): lax.ppermute(v, 'dp', [(a * inner + i, b * inner + i) for a, b in pairs f...  75.5 us
    dot_general x46, matrix products, dot(): return lax.dot_general(a, b, dims, preferred_element_type=F32)  55.9 us
    ppermute x13, waiting for transfers between devices, dp_sum(): other = lax.ppermute(value, 'dp', pairs)  33.6 us
    ppermute x13, waiting for transfers between devices, dp_sum(): came = lax.ppermute(sent, 'dp', pairs)  33.3 us
    ppermute x29, waiting for transfers between devices, tensor_send(): return lax.ppermute(value, 'tensor', [(i, i ^ flip) for i in range(4)])  26.3 us
    ppermute x29, starting transfers between devices, tensor_send(): return lax.ppermute(value, 'tensor', [(i, i ^ flip) for i in range(4)])  16.2 us
    ppermute x13, starting transfers between devices, dp_sum(): came = lax.ppermute(sent, 'dp', pairs)  14.4 us
  transfers between devices with their start and end apart: 97, of which 46 were waited for; matrix products, arithmetic and copies ran while one was open for 21% of the time, Pallas kernels for 4%

profile of v1, /device:TPU:0, one launch (start us, length us, event | category | flops | bytes accessed | tf_op | source)
XLA Modules:
  0.0 499.1 jit_solution(16498957684115196932)
XLA Ops:
  5.9 11.2 %collective-permute-done.1 = bf16[256,1024]{0,1:T(8,128)(2,1)} collective-permute-done((bf16[256,1024]{0,1:T(8,128)(2,1)S(1)}, bf16[256,1024]{0,1:T(8,128)(2,1)}, u32[]{:S(2)}, u32[]{:S(2)}) %collective-permute-start.1) | collective-permute-done | bytes 524320 | tf_op jit(solution)/shard_map/ppermute | solution.py:261
  25.8 4.7 collective-permute-done.7
  44.8 8.5 %attend_forward.1 = (bf16[1024,256]{1,0:T(8,128)(2,1)S(1)}, f32[1024,256]{1,0:T(8,128)S(1)}) custom-call(s32[1]{0:T(128)S(6)} %copy.123.prefix_ref, f32[4]{0:T(128)S(1)} %multiply_power_fusion.slope_ref, bf16[1024,768]{1,0:T(8,128)(2,1)S(1)} %add_convert_fusion.1.joined_ref), custom_call_target="tpu_custom_call" | custom-call | flops 2147483648 | bytes 4194304 | tf_op jit(solution)/shard_map/attend_forward/pallas_call | solution.py:140
  58.5 7.6 %collective-permute-done.4 = bf16[1024,256]{1,0:T(8,128)(2,1)} collective-permute-done((bf16[1024,256]{1,0:T(8,128)(2,1)S(1)}, bf16[1024,256]{1,0:T(8,128)(2,1)}, u32[]{:S(2)}, u32[]{:S(2)}) %collective-permute-start.4) | collective-permute-done | bytes 524320 | tf_op jit(solution)/shard_map/ppermute | solution.py:261
  70.9 4.8 fusion.158
  80.9 5.5 %convert_reduce_fusion.1 = (f32[1024]{0:T(1024)}, bf16[1024,1024]{1,0:T(8,128)(2,1)S(1)}) fusion(f32[1024,1024]{1,0:T(8,128)S(1)} %get-tuple-element.88, f32[1024]{0:T(1024)S(1)} %copy-done.45, bf16[1024,1024]{0,1:T(8,128)(2,1)S(1)} %constant_dynamic-update-slice_fusion.7, bf16[1024,1024]{1,0:T(8,128)(2,1)S(1)} %copy-done.23), kind=kOutput, calls=%fused_computation.18 | convolution fusion | flops 2170551296 | bytes 10493952 | tf_op jit(solution)/shard_map/dot_general | solution.py:22
  103.4 20.0 %collective-permute-done.92 = bf16[128,1024]{1,0:T(8,128)(2,1)S(1)} collective-permute-done((bf16[128,1024]{1,0:T(8,128)(2,1)S(1)}, bf16[128,1024]{1,0:T(8,128)(2,1)S(1)}, u32[]{:S(2)}, u32[]{:S(2)}) %collective-permute-start.92) | collective-permute-done | bytes 262176 | tf_op jit(solution)/shard_map/ppermute | solution.py:319
  151.0 4.4 collective-permute-start.88
  156.6 4.4 collective-permute-start.93
  162.2 4.4 collective-permute-start.73
  167.8 4.4 collective-permute-start.58
  173.4 4.4 collective-permute-start.63
  179.1 4.4 collective-permute-start.68
  184.7 5.2 %collective-permute-done.68 = bf16[128,1024]{1,0:T(8,128)(2,1)S(1)} collective-permute-done((bf16[128,1024]{1,0:T(8,128)(2,1)S(1)}, bf16[128,1024]{1,0:T(8,128)(2,1)S(1)}, u32[]{:S(2)}, u32[]{:S(2)}) %collective-permute-start.68) | collective-permute-done | bytes 262176 | tf_op jit(solution)/shard_map/ppermute | solution.py:294
  201.8 35.7 %collective-permute-done.80 = bf16[128,1024]{1,0:T(8,128)(2,1)S(1)} collective-permute-done((bf16[128,1024]{1,0:T(8,128)(2,1)S(1)}, bf16[128,1024]{1,0:T(8,128)(2,1)S(1)}, u32[]{:S(2)}, u32[]{:S(2)}) %collective-permute-start.80) | collective-permute-done | bytes 262176 | tf_op jit(solution)/shard_map/ppermute | solution.py:294
  245.1 4.9 collective-permute-done.90
  256.9 4.3 collective-permute-done.75
  262.5 4.3 collective-permute-done.60
  273.7 5.8 %collective-permute-done.70 = bf16[128,1024]{1,0:T(8,128)(2,1)S(1)} collective-permute-done((bf16[128,1024]{1,0:T(8,128)(2,1)S(1)}, bf16[128,1024]{1,0:T(8,128)(2,1)S(1)}, u32[]{:S(2)}, u32[]{:S(2)}) %collective-permute-start.70) | collective-permute-done | bytes 262176 | tf_op jit(solution)/shard_map/ppermute | solution.py:294
  303.1 12.0 %attend_backward.1 = bf16[1024,768]{1,0:T(8,128)(2,1)S(1)} custom-call(s32[1]{0:T(128)S(6)} %copy.123.prefix_ref, f32[4]{0:T(128)S(1)} %multiply_power_fusion.slope_ref, bf16[1024,768]{1,0:T(8,128)(2,1)S(1)} %copy-done.4, f32[1024,256]{1,0:T(8,128)S(1)} %copy-done.6, bf16[1024,256]{1,0:T(8,128)(2,1)S(1)} %get-tuple-element.20.context_ref, ...), custom_call_target="tpu_custom_call" | custom-call | flops 5368709120 | bytes 6291456 | tf_op jit(solution)/shard_map/attend_backward/pallas_call | solution.py:239
  329.8 5.9 %collective-permute-done.66 = bf16[128,1024]{1,0:T(8,128)(2,1)S(1)} collective-permute-done((bf16[128,1024]{1,0:T(8,128)(2,1)S(1)}, bf16[128,1024]{1,0:T(8,128)(2,1)S(1)}, u32[]{:S(2)}, u32[]{:S(2)}) %collective-permute-start.66) | collective-permute-done | bytes 262176 | tf_op jit(solution)/shard_map/ppermute | solution.py:322
  336.9 6.0 %collective-permute-done.71 = bf16[128,1024]{1,0:T(8,128)(2,1)S(1)} collective-permute-done((bf16[128,1024]{1,0:T(8,128)(2,1)S(1)}, bf16[128,1024]{1,0:T(8,128)(2,1)S(1)}, u32[]{:S(2)}, u32[]{:S(2)}) %collective-permute-start.71) | collective-permute-done | bytes 262176 | tf_op jit(solution)/shard_map/ppermute | solution.py:322
  344.0 5.2 %collective-permute-done.76 = bf16[128,1024]{1,0:T(8,128)(2,1)S(1)} collective-permute-done((bf16[128,1024]{1,0:T(8,128)(2,1)S(1)}, bf16[128,1024]{1,0:T(8,128)(2,1)S(1)}, u32[]{:S(2)}, u32[]{:S(2)}) %collective-permute-start.76) | collective-permute-done | bytes 262176 | tf_op jit(solution)/shard_map/ppermute | solution.py:322
  377.5 4.4 collective-permute-start.30
  385.0 4.4 collective-permute-start.35
  392.6 4.4 collective-permute-start.40
  407.6 17.5 %collective-permute-done.27 = bf16[128,768]{1,0:T(8,128)(2,1)S(1)} collective-permute-done((bf16[128,768]{1,0:T(8,128)(2,1)S(1)}, bf16[128,768]{1,0:T(8,128)(2,1)S(1)}, u32[]{:S(2)}, u32[]{:S(2)}) %collective-permute-start.27) | collective-permute-done | bytes 196640 | tf_op jit(solution)/shard_map/ppermute | solution.py:294
  430.5 3.8 collective-permute-done.37
  437.5 4.6 collective-permute-done.28
  467.1 5.1 %collective-permute-done.45 = f32[9,1024]{1,0:T(8,128)S(1)} collective-permute-done((f32[9,1024]{1,0:T(8,128)S(1)}, f32[9,1024]{1,0:T(8,128)S(1)}, u32[]{:S(2)}, u32[]{:S(2)}) %collective-permute-start.45) | collective-permute-done | bytes 36896 | tf_op jit(solution)/shard_map/ppermute | solution.py:333
  485.8 5.3 %collective-permute-done.53 = bf16[128,1024]{1,0:T(8,128)(2,1)S(1)} collective-permute-done((bf16[128,1024]{1,0:T(8,128)(2,1)S(1)}, bf16[128,1024]{1,0:T(8,128)(2,1)S(1)}, u32[]{:S(2)}, u32[]{:S(2)}) %collective-permute-start.53) | collective-permute-done | bytes 262176 | tf_op jit(solution)/shard_map/ppermute | solution.py:294
  493.2 4.3 collective-permute-done.54
  (443 shorter events, 264.0 us)
Async XLA Ops:
  5.1 17.0 %collective-permute-start = (bf16[256,1024]{0,1:T(8,128)(2,1)S(1)}, bf16[256,1024]{0,1:T(8,128)(2,1)}, u32[]{:S(2)}, u32[]{:S(2)}) collective-permute-start(bf16[256,1024]{0,1:T(8,128)(2,1)S(1)} %copy.52), channel_id=1, source_target_pairs={{0,1},{1,0},{2,3},{3,2},{4,5},{5,4},{6,7},{7,6},{8,9},{9,8},{10,11... | collective-permute-start | bytes 1572872 | tf_op jit(solution)/shard_map/ppermute | solution.py:261
  31.5 26.5 %collective-permute-start.13 = (bf16[256,1024]{0,1:T(8,128)(2,1)}, bf16[256,1024]{0,1:T(8,128)(2,1)}, u32[]{:S(2)}, u32[]{:S(2)}) collective-permute-start(bf16[256,1024]{0,1:T(8,128)(2,1)} %copy.60), channel_id=1, source_target_pairs={{0,2},{1,3},{2,0},{3,1},{4,6},{5,7},{6,4},{7,5},{8,10},{9,11},{10,... | collective-permute-start | bytes 1572872 | tf_op jit(solution)/shard_map/ppermute | solution.py:261
  97.3 33.7 %collective-permute-start.77 = (bf16[128,1024]{1,0:T(8,128)(2,1)S(1)}, bf16[128,1024]{1,0:T(8,128)(2,1)S(1)}, u32[]{:S(2)}, u32[]{:S(2)}) collective-permute-start(bf16[128,1024]{1,0:T(8,128)(2,1)S(1)} %convolution_convert_fusion.9), channel_id=1, source_target_pairs={{0,4},{4,0},{8,12},{12,8},{16,20},{20,16},{24,28},{28,24},{1,5},{5... | collective-permute-start | bytes 786440 | tf_op jit(solution)/shard_map/ppermute | solution.py:319
  98.9 36.2 %collective-permute-start.82 = (bf16[128,1024]{1,0:T(8,128)(2,1)S(1)}, bf16[128,1024]{1,0:T(8,128)(2,1)S(1)}, u32[]{:S(2)}, u32[]{:S(2)}) collective-permute-start(bf16[128,1024]{1,0:T(8,128)(2,1)S(1)} %convolution_convert_fusion.8), channel_id=1, source_target_pairs={{0,4},{4,0},{8,12},{12,8},{16,20},{20,16},{24,28},{28,24},{1,5},{5... | collective-permute-start | bytes 786440 | tf_op jit(solution)/shard_map/ppermute | solution.py:319
  99.4 41.5 %collective-permute-start.87 = (bf16[128,1024]{1,0:T(8,128)(2,1)S(1)}, bf16[128,1024]{1,0:T(8,128)(2,1)S(1)}, u32[]{:S(2)}, u32[]{:S(2)}) collective-permute-start(bf16[128,1024]{1,0:T(8,128)(2,1)S(1)} %convolution_convert_fusion.7), channel_id=1, source_target_pairs={{0,4},{4,0},{8,12},{12,8},{16,20},{20,16},{24,28},{28,24},{1,5},{5... | collective-permute-start | bytes 786440 | tf_op jit(solution)/shard_map/ppermute | solution.py:319
  100.9 22.5 %collective-permute-start.92 = (bf16[128,1024]{1,0:T(8,128)(2,1)S(1)}, bf16[128,1024]{1,0:T(8,128)(2,1)S(1)}, u32[]{:S(2)}, u32[]{:S(2)}) collective-permute-start(bf16[128,1024]{1,0:T(8,128)(2,1)S(1)} %convolution_convert_fusion.6), channel_id=1, source_target_pairs={{0,4},{4,0},{8,12},{12,8},{16,20},{20,16},{24,28},{28,24},{1,5},{5... | collective-permute-start | bytes 786440 | tf_op jit(solution)/shard_map/ppermute | solution.py:319
  101.4 27.6 %collective-permute-start.72 = (bf16[128,1024]{1,0:T(8,128)(2,1)S(1)}, bf16[128,1024]{1,0:T(8,128)(2,1)S(1)}, u32[]{:S(2)}, u32[]{:S(2)}) collective-permute-start(bf16[128,1024]{1,0:T(8,128)(2,1)S(1)} %convolution_convert_fusion.10), channel_id=1, source_target_pairs={{0,4},{4,0},{8,12},{12,8},{16,20},{20,16},{24,28},{28,24},{1,5},{5... | collective-permute-start | bytes 786440 | tf_op jit(solution)/shard_map/ppermute | solution.py:319
  134.6 147.2 %collective-permute-start.9 = (bf16[256,1024]{0,1:T(8,128)(2,1)S(1)}, bf16[256,1024]{0,1:T(8,128)(2,1)S(1)}, u32[]{:S(2)}, u32[]{:S(2)}) collective-permute-start(bf16[256,1024]{0,1:T(8,128)(2,1)S(1)} %convolution_convert_fusion.3), channel_id=1, source_target_pairs={{0,1},{1,0},{2,3},{3,2},{4,5},{5,4},{6,7},{7,6},{8,9},{9,8},{10,11... | collective-permute-start | bytes 1572872 | tf_op jit(solution)/shard_map/ppermute | solution.py:261
  135.1 55.6 %collective-permute-start.10 = (bf16[256,1024]{0,1:T(8,128)(2,1)S(1)}, bf16[256,1024]{0,1:T(8,128)(2,1)S(1)}, u32[]{:S(2)}, u32[]{:S(2)}) collective-permute-start(bf16[256,1024]{0,1:T(8,128)(2,1)S(1)} %convolution_convert_fusion.2), channel_id=1, source_target_pairs={{0,1},{1,0},{2,3},{3,2},{4,5},{5,4},{6,7},{7,6},{8,9},{9,8},{10,11... | collective-permute-start | bytes 1572872 | tf_op jit(solution)/shard_map/ppermute | solution.py:261
  140.2 142.0 %collective-permute-start.15 = (bf16[256,1024]{0,1:T(8,128)(2,1)S(1)}, bf16[256,1024]{0,1:T(8,128)(2,1)S(1)}, u32[]{:S(2)}, u32[]{:S(2)}) collective-permute-start(bf16[256,1024]{0,1:T(8,128)(2,1)S(1)} %convolution_convert_fusion.1), channel_id=1, source_target_pairs={{0,1},{1,0},{2,3},{3,2},{4,5},{5,4},{6,7},{7,6},{8,9},{9,8},{10,11... | collective-permute-start | bytes 1572872 | tf_op jit(solution)/shard_map/ppermute | solution.py:261
  197.6 39.8 %collective-permute-start.80 = (bf16[128,1024]{1,0:T(8,128)(2,1)S(1)}, bf16[128,1024]{1,0:T(8,128)(2,1)S(1)}, u32[]{:S(2)}, u32[]{:S(2)}) collective-permute-start(bf16[128,1024]{1,0:T(8,128)(2,1)S(1)} %add_convert_fusion.10), channel_id=1, source_target_pairs={{8,0},{12,4},{16,24},{20,28},{9,1},{13,5},{17,25},{21,29},{10,2},{... | collective-permute-start | bytes 786440 | tf_op jit(solution)/shard_map/ppermute | solution.py:294
  199.0 44.0 %collective-permute-start.85 = (bf16[128,1024]{1,0:T(8,128)(2,1)S(1)}, bf16[128,1024]{1,0:T(8,128)(2,1)S(1)}, u32[]{:S(2)}, u32[]{:S(2)}) collective-permute-start(bf16[128,1024]{1,0:T(8,128)(2,1)S(1)} %add_convert_fusion.8), channel_id=1, source_target_pairs={{8,0},{12,4},{16,24},{20,28},{9,1},{13,5},{17,25},{21,29},{10,2},{... | collective-permute-start | bytes 786440 | tf_op jit(solution)/shard_map/ppermute | solution.py:294
  200.4 49.6 %collective-permute-start.90 = (bf16[128,1024]{1,0:T(8,128)(2,1)S(1)}, bf16[128,1024]{1,0:T(8,128)(2,1)S(1)}, u32[]{:S(2)}, u32[]{:S(2)}) collective-permute-start(bf16[128,1024]{1,0:T(8,128)(2,1)S(1)} %add_convert_fusion.6), channel_id=1, source_target_pairs={{8,0},{12,4},{16,24},{20,28},{9,1},{13,5},{17,25},{21,29},{10,2},{... | collective-permute-start | bytes 786440 | tf_op jit(solution)/shard_map/ppermute | solution.py:294
  237.4 18.2 %collective-permute-start.95 = (bf16[128,1024]{1,0:T(8,128)(2,1)S(1)}, bf16[128,1024]{1,0:T(8,128)(2,1)S(1)}, u32[]{:S(2)}, u32[]{:S(2)}) collective-permute-start(bf16[128,1024]{1,0:T(8,128)(2,1)S(1)} %add_convert_fusion.4), channel_id=1, source_target_pairs={{8,0},{12,4},{16,24},{20,28},{9,1},{13,5},{17,25},{21,29},{10,2},{... | collective-permute-start | bytes 786440 | tf_op jit(solution)/shard_map/ppermute | solution.py:294
  243.1 18.2 %collective-permute-start.75 = (bf16[128,1024]{1,0:T(8,128)(2,1)S(1)}, bf16[128,1024]{1,0:T(8,128)(2,1)S(1)}, u32[]{:S(2)}, u32[]{:S(2)}) collective-permute-start(bf16[128,1024]{1,0:T(8,128)(2,1)S(1)} %add_convert_fusion.12), channel_id=1, source_target_pairs={{8,0},{12,4},{16,24},{20,28},{9,1},{13,5},{17,25},{21,29},{10,2},{... | collective-permute-start | bytes 786440 | tf_op jit(solution)/shard_map/ppermute | solution.py:294
  250.0 16.9 %collective-permute-start.60 = (bf16[128,1024]{1,0:T(8,128)(2,1)S(1)}, bf16[128,1024]{1,0:T(8,128)(2,1)S(1)}, u32[]{:S(2)}, u32[]{:S(2)}) collective-permute-start(bf16[128,1024]{1,0:T(8,128)(2,1)S(1)} %add_convert_fusion.21), channel_id=1, source_target_pairs={{8,0},{12,4},{16,24},{20,28},{9,1},{13,5},{17,25},{21,29},{10,2},{... | collective-permute-start | bytes 786440 | tf_op jit(solution)/shard_map/ppermute | solution.py:294
  255.6 15.3 %collective-permute-start.65 = (bf16[128,1024]{1,0:T(8,128)(2,1)S(1)}, bf16[128,1024]{1,0:T(8,128)(2,1)S(1)}, u32[]{:S(2)}, u32[]{:S(2)}) collective-permute-start(bf16[128,1024]{1,0:T(8,128)(2,1)S(1)} %add_convert_fusion.18), channel_id=1, source_target_pairs={{8,0},{12,4},{16,24},{20,28},{9,1},{13,5},{17,25},{21,29},{10,2},{... | collective-permute-start | bytes 786440 | tf_op jit(solution)/shard_map/ppermute | solution.py:294
  261.2 22.6 %collective-permute-start.11 = (bf16[256,1024]{0,1:T(8,128)(2,1)S(1)}, bf16[256,1024]{0,1:T(8,128)(2,1)S(1)}, u32[]{:S(2)}, u32[]{:S(2)}) collective-permute-start(bf16[256,1024]{0,1:T(8,128)(2,1)S(1)} %add_convert_fusion.3), channel_id=1, source_target_pairs={{0,2},{1,3},{2,0},{3,1},{4,6},{5,7},{6,4},{7,5},{8,10},{9,11},{10,... | collective-permute-start | bytes 1572872 | tf_op jit(solution)/shard_map/ppermute | solution.py:261
  266.9 17.0 %collective-permute-start.17 = (bf16[256,1024]{0,1:T(8,128)(2,1)S(1)}, bf16[256,1024]{0,1:T(8,128)(2,1)S(1)}, u32[]{:S(2)}, u32[]{:S(2)}) collective-permute-start(bf16[256,1024]{0,1:T(8,128)(2,1)S(1)} %add_convert_fusion.2), channel_id=1, source_target_pairs={{0,2},{1,3},{2,0},{3,1},{4,6},{5,7},{6,4},{7,5},{8,10},{9,11},{10,... | collective-permute-start | bytes 1572872 | tf_op jit(solution)/shard_map/ppermute | solution.py:261
  279.5 71.1 %collective-permute-start.81 = (bf16[128,1024]{1,0:T(8,128)(2,1)}, bf16[128,1024]{1,0:T(8,128)(2,1)}, u32[]{:S(2)}, u32[]{:S(2)}) collective-permute-start(bf16[128,1024]{1,0:T(8,128)(2,1)} %broadcast_select_fusion.3), channel_id=1, source_target_pairs={{0,4},{4,0},{8,12},{12,8},{16,20},{20,16},{24,28},{28,24},{1,5},{5... | collective-permute-start | bytes 786440 | tf_op jit(solution)/shard_map/ppermute | solution.py:322
  281.8 70.9 %collective-permute-start.86 = (bf16[128,1024]{1,0:T(8,128)(2,1)}, bf16[128,1024]{1,0:T(8,128)(2,1)}, u32[]{:S(2)}, u32[]{:S(2)}) collective-permute-start(bf16[128,1024]{1,0:T(8,128)(2,1)} %broadcast_select_fusion.2), channel_id=1, source_target_pairs={{0,4},{4,0},{8,12},{12,8},{16,20},{20,16},{24,28},{28,24},{1,5},{5... | collective-permute-start | bytes 786440 | tf_op jit(solution)/shard_map/ppermute | solution.py:322
  282.3 73.7 %collective-permute-start.91 = (bf16[128,1024]{1,0:T(8,128)(2,1)}, bf16[128,1024]{1,0:T(8,128)(2,1)}, u32[]{:S(2)}, u32[]{:S(2)}) collective-permute-start(bf16[128,1024]{1,0:T(8,128)(2,1)} %broadcast_select_fusion.1), channel_id=1, source_target_pairs={{0,4},{4,0},{8,12},{12,8},{16,20},{20,16},{24,28},{28,24},{1,5},{5... | collective-permute-start | bytes 786440 | tf_op jit(solution)/shard_map/ppermute | solution.py:322
  297.1 64.4 %collective-permute-start.96 = (bf16[128,1024]{1,0:T(8,128)(2,1)S(1)}, bf16[128,1024]{1,0:T(8,128)(2,1)}, u32[]{:S(2)}, u32[]{:S(2)}) collective-permute-start(bf16[128,1024]{1,0:T(8,128)(2,1)S(1)} %broadcast_select_fusion), channel_id=1, source_target_pairs={{0,4},{4,0},{8,12},{12,8},{16,20},{20,16},{24,28},{28,24},{1,5},{5... | collective-permute-start | bytes 786440 | tf_op jit(solution)/shard_map/ppermute | solution.py:322
  299.5 28.0 %collective-permute-start.61 = (bf16[128,1024]{1,0:T(8,128)(2,1)}, bf16[128,1024]{1,0:T(8,128)(2,1)}, u32[]{:S(2)}, u32[]{:S(2)}) collective-permute-start(bf16[128,1024]{1,0:T(8,128)(2,1)} %broadcast_select_fusion.7), channel_id=1, source_target_pairs={{0,4},{4,0},{8,12},{12,8},{16,20},{20,16},{24,28},{28,24},{1,5},{5... | collective-permute-start | bytes 786440 | tf_op jit(solution)/shard_map/ppermute | solution.py:322
  349.2 53.8 %collective-permute-start.48 = (bf16[256,1024]{0,1:T(8,128)(2,1)S(1)}, bf16[256,1024]{0,1:T(8,128)(2,1)S(1)}, u32[]{:S(2)}, u32[]{:S(2)}) collective-permute-start(bf16[256,1024]{0,1:T(8,128)(2,1)S(1)} %copy-done.9), channel_id=1, source_target_pairs={{0,2},{1,3},{2,0},{3,1},{4,6},{5,7},{6,4},{7,5},{8,10},{9,11},{10,... | collective-permute-start | bytes 1572872 | tf_op jit(solution)/shard_map/ppermute | solution.py:261
  350.6 51.7 %collective-permute-start.47 = (bf16[256,1024]{0,1:T(8,128)(2,1)S(1)}, bf16[256,1024]{0,1:T(8,128)(2,1)S(1)}, u32[]{:S(2)}, u32[]{:S(2)}) collective-permute-start(bf16[256,1024]{0,1:T(8,128)(2,1)S(1)} %copy-done.9), channel_id=1, source_target_pairs={{0,1},{1,0},{2,3},{3,2},{4,5},{5,4},{6,7},{7,6},{8,9},{9,8},{10,11... | collective-permute-start | bytes 1572872 | tf_op jit(solution)/shard_map/ppermute | solution.py:261
  367.8 88.8 %collective-permute-start.21 = (bf16[256,1024]{0,1:T(8,128)(2,1)S(1)}, bf16[256,1024]{0,1:T(8,128)(2,1)S(1)}, u32[]{:S(2)}, u32[]{:S(2)}) collective-permute-start(bf16[256,1024]{0,1:T(8,128)(2,1)S(1)} %copy-done.28), channel_id=1, source_target_pairs={{0,1},{1,0},{2,3},{3,2},{4,5},{5,4},{6,7},{7,6},{8,9},{9,8},{10,11... | collective-permute-start | bytes 1572872 | tf_op jit(solution)/shard_map/ppermute | solution.py:261
  368.5 32.4 %collective-permute-start.22 = (bf16[256,1024]{0,1:T(8,128)(2,1)S(1)}, bf16[256,1024]{0,1:T(8,128)(2,1)S(1)}, u32[]{:S(2)}, u32[]{:S(2)}) collective-permute-start(bf16[256,1024]{0,1:T(8,128)(2,1)S(1)} %copy-done.29), channel_id=1, source_target_pairs={{0,1},{1,0},{2,3},{3,2},{4,5},{5,4},{6,7},{7,6},{8,9},{9,8},{10,11... | collective-permute-start | bytes 1572872 | tf_op jit(solution)/shard_map/ppermute | solution.py:261
  403.8 52.8 %collective-permute-start.23 = (bf16[256,1024]{0,1:T(8,128)(2,1)S(1)}, bf16[256,1024]{0,1:T(8,128)(2,1)S(1)}, u32[]{:S(2)}, u32[]{:S(2)}) collective-permute-start(bf16[256,1024]{0,1:T(8,128)(2,1)S(1)} %fusion.33), channel_id=1, source_target_pairs={{0,2},{1,3},{2,0},{3,1},{4,6},{5,7},{6,4},{7,5},{8,10},{9,11},{10,... | collective-permute-start | bytes 1572872 | tf_op jit(solution)/shard_map/ppermute | solution.py:261
  404.7 49.3 %collective-permute-start.49 = (bf16[256,1024]{0,1:T(8,128)(2,1)S(1)}, bf16[256,1024]{0,1:T(8,128)(2,1)S(1)}, u32[]{:S(2)}, u32[]{:S(2)}) collective-permute-start(bf16[256,1024]{0,1:T(8,128)(2,1)S(1)} %collective-permute-done.48), channel_id=1, source_target_pairs={{0,1},{1,0},{2,3},{3,2},{4,5},{5,4},{6,7},{7,6},{8,9},{9,8},{10,11... | collective-permute-start | bytes 1572872 | tf_op jit(solution)/shard_map/ppermute | solution.py:261
  404.8 20.3 %collective-permute-start.27 = (bf16[128,768]{1,0:T(8,128)(2,1)S(1)}, bf16[128,768]{1,0:T(8,128)(2,1)S(1)}, u32[]{:S(2)}, u32[]{:S(2)}) collective-permute-start(bf16[128,768]{1,0:T(8,128)(2,1)S(1)} %add_convert_fusion.32), channel_id=1, source_target_pairs={{8,0},{12,4},{16,24},{20,28},{9,1},{13,5},{17,25},{21,29},{10,2},{... | collective-permute-start | bytes 589832 | tf_op jit(solution)/shard_map/ppermute | solution.py:294
  406.2 22.7 %collective-permute-start.32 = (bf16[128,768]{1,0:T(8,128)(2,1)S(1)}, bf16[128,768]{1,0:T(8,128)(2,1)S(1)}, u32[]{:S(2)}, u32[]{:S(2)}) collective-permute-start(bf16[128,768]{1,0:T(8,128)(2,1)S(1)} %add_convert_fusion.30), channel_id=1, source_target_pairs={{8,0},{12,4},{16,24},{20,28},{9,1},{13,5},{17,25},{21,29},{10,2},{... | collective-permute-start | bytes 589832 | tf_op jit(solution)/shard_map/ppermute | solution.py:294
  (111 other events, 914.2 us)

commit v2 on v1

v2 whole, which is shorter than its diff:
```python
from functools import partial

import jax
import jax.numpy as jnp
from jax import lax
from jax.experimental import pallas as pl
from jax.experimental.pallas import tpu as pltpu
from jax.sharding import PartitionSpec as P

HEADS = 16
PREFIX_MOST = 512

epsilon = 1e-05
BF = jnp.bfloat16
F32 = jnp.float32
NT = (((1,), (1,)), ((), ()))
NN = (((1,), (0,)), ((), ()))
TN = (((0,), (0,)), ((), ()))


def dot(a, b, dims):
    return lax.dot_general(a, b, dims, preferred_element_type=F32)


def after(value, *others):
    return lax.optimization_barrier((value,) + others)[0]


def norm_parts(values):
    center = jnp.mean(values, axis=-1, keepdims=True)
    deviation = values - center
    variance = jnp.mean(deviation * deviation, axis=-1, keepdims=True)
    rstd = lax.rsqrt(variance + epsilon)
    return deviation * rstd, rstd


def norm_backward(values, gain, upstream):
    unit, rstd = norm_parts(values)
    scaled = upstream * gain
    grad = rstd * (
        scaled
        - jnp.mean(scaled, axis=-1, keepdims=True)
        - unit * jnp.mean(scaled * unit, axis=-1, keepdims=True)
    )
    return grad, jnp.sum(upstream * unit, axis=0), jnp.sum(upstream, axis=0)


def split3(value):
    high = value.astype(BF).astype(F32)
    rest = value - high
    mid = rest.astype(BF).astype(F32)
    return high, mid, rest - mid


def place(lane, base, items):
    out = jnp.zeros(lane.shape, F32)
    for i, item in enumerate(items):
        out = jnp.where(lane == base + i, item, out)
    return out


def causal_end(row_block, size, length):
    return min(max((row_block + 1) * size, min(PREFIX_MOST, length)), length)


def fill_masks(masks, prefix, size, blocks, transposed):
    shape = (size, size)
    for index, (row_block, col_block) in enumerate(blocks):
        rows = row_block * size + lax.broadcasted_iota(jnp.int32, shape, 1 if transposed else 0)
        cols = col_block * size + lax.broadcasted_iota(jnp.int32, shape, 0 if transposed else 1)
        allowed = (cols <= rows) | ((cols < prefix) & (rows < prefix))
        beyond = jnp.maximum(cols - rows, 0).astype(F32)
        masks[index] = jnp.where(allowed, -2.0 * beyond, -1e30)


def special_blocks(length, size):
    out = []
    for row_block in range(length // size):
        for col_block in range(causal_end(row_block, size, length) // size):
            if col_block >= row_block:
                out.append((row_block, col_block))
    return out


def load_order(me_ref, near_ref, far_ref, joined_ref):
    half = near_ref.shape[0]
    chip = me_ref[0] >> 1
    joined_ref[pl.ds(pl.multiple_of(chip * half, half), half), :] = near_ref[...]
    joined_ref[pl.ds(pl.multiple_of((1 - chip) * half, half), half), :] = far_ref[...]


def attend_forward_kernel(size, prefix_ref, slope_ref, me_ref, near_ref, far_ref, context_ref, total_ref, masks, joined_ref):
    length = joined_ref.shape[0]
    pair = pl.program_id(0)
    load_order(me_ref, near_ref, far_ref, joined_ref)
    blocks = special_blocks(length, size)

    @pl.when(pair == 0)
    def _():
        fill_masks(masks, prefix_ref[0], size, blocks, False)

    lane = lax.broadcasted_iota(jnp.int32, (length, 128), 1)
    low = lane < 64
    position = lax.broadcasted_iota(jnp.int32, (length, 1), 0).astype(F32)
    tiles = [joined_ref[:, i * 128 : (i + 1) * 128].astype(F32) for i in range(3)]
    rolled0 = pltpu.roll(tiles[0], 64, 1)
    rolled1 = pltpu.roll(tiles[1], 64, 1)
    sides = []
    for head in range(2):
        slope = slope_ref[pair * 2 + head]
        own = jnp.logical_not(low) if head == 0 else low
        base = 0 if head == 0 else 64
        query = jnp.where(own, (rolled0 if head == 0 else rolled1) * 0.125, place(lane, base, (1.0, 1.0, 1.0)))
        keys = jnp.where(own, tiles[0] if head == 0 else tiles[2], place(lane, base, split3(slope * position)))
        value = jnp.where(low, tiles[1], 1.0) if head == 0 else jnp.where(low, 1.0, tiles[2])
        sides.append((slope, query.astype(BF), keys.astype(BF), value.astype(BF)))
    low_block = low[:size]
    lane_block = lane[:size]
    for row_block in range(length // size):
        end = causal_end(row_block, size, length)
        rows = slice(row_block * size, (row_block + 1) * size)
        results = []
        for head in range(2):
            slope, query, keys, value = sides[head]
            scores = dot(query[rows], keys[:end], NT)
            columns = []
            for col_block in range(end // size):
                piece = scores[:, col_block * size : (col_block + 1) * size]
                if col_block >= row_block:
                    piece = piece + slope * masks[blocks.index((row_block, col_block))]
                columns.append(piece)
            highest = columns[0]
            for piece in columns[1:]:
                highest = jnp.maximum(highest, piece)
            highest = jnp.max(highest, axis=-1, keepdims=True)
            powered = jnp.concatenate([jnp.exp(piece - highest).astype(BF) for piece in columns], axis=1)
            gathered = dot(powered, value[:end], NN)
            total = gathered[:, 64:65] if head == 0 else gathered[:, 0:1]
            results.append((gathered / total, highest + jnp.log(total)))
        context_ref[rows, :] = jnp.where(low_block, results[0][0], results[1][0]).astype(BF)
        total_ref[rows, :] = jnp.where(lane_block == 0, results[0][1], results[1][1])


def attend_forward(near, far, prefix, slopes, me, pair, size=256):
    length = 2 * near.shape[0]
    count = len(special_blocks(length, size))
    tile = pl.BlockSpec((length, 128), lambda p, *_: (0, 0))
    return pl.pallas_call(
        partial(attend_forward_kernel, size),
        grid_spec=pltpu.PrefetchScalarGridSpec(
            num_scalar_prefetch=3,
            grid=(1,),
            in_specs=[pl.BlockSpec((length // 2, 384), lambda p, *_: (0, pair))] * 2,
            out_specs=[tile, tile],
            scratch_shapes=[pltpu.VMEM((count, size, size), F32), pltpu.VMEM((length, 384), BF)],
        ),
        out_shape=[jax.ShapeDtypeStruct((length, 128), BF), jax.ShapeDtypeStruct((length, 128), F32)],
        compiler_params=pltpu.CompilerParams(vmem_limit_bytes=40 * 1024 * 1024),
        cost_estimate=pl.CostEstimate(flops=2 * 2 * 2 * length * length * 128, bytes_accessed=2 * 1024 * 1024, transcendentals=0),
        name="attend_forward",
    )(prefix, slopes[2 * pair : 2 * pair + 2], me, near, far)


def attend_backward_kernel(
    size, prefix_ref, slope_ref, me_ref, near_ref, far_ref, total_ref, context_ref, g0, g1, g2, g3,
    final_ref, masks, query_sum, grad_ref, joined_ref, out_ref,
):
    length = joined_ref.shape[0]
    pair = pl.program_id(0)
    load_order(me_ref, near_ref, far_ref, joined_ref)
    rows = g0.shape[0]
    for flip, ref in enumerate((g0, g1, g2, g3)):
        grad_ref[pl.ds(pl.multiple_of((me_ref[0] ^ flip) * rows, rows), rows), :] = ref[...]
    totals = total_ref[...]
    blocks = special_blocks(length, size)

    @pl.when(pair == 0)
    def _():
        fill_masks(masks, prefix_ref[0], size, blocks, True)

    lane = lax.broadcasted_iota(jnp.int32, (length, 128), 1)
    low = lane < 64
    position = lax.broadcasted_iota(jnp.int32, (length, 1), 0).astype(F32)
    tiles = [joined_ref[:, i * 128 : (i + 1) * 128].astype(F32) for i in range(3)]
    rolled = [pltpu.roll(tile, 64, 1) for tile in tiles]
    grad = grad_ref[...].astype(F32)
    product = grad * context_ref[...].astype(F32)
    grad_low = grad.astype(BF)
    rolled_low = [tile.astype(BF) for tile in rolled]
    sides = []
    for head in range(2):
        slope = slope_ref[pair * 2 + head]
        own = jnp.logical_not(low) if head == 0 else low
        base = 0 if head == 0 else 64
        log_total = totals[:, head : head + 1]
        query = jnp.where(
            own, rolled[head] * 0.125, place(lane, base, (1.0, 1.0, 1.0) + split3(log_total))
        )
        keys = jnp.where(
            own, tiles[0] if head == 0 else tiles[2], place(lane, base, split3(slope * position) + (-1.0, -1.0, -1.0))
        )
        head_lanes = low if head == 0 else jnp.logical_not(low)
        inner = jnp.sum(jnp.where(head_lanes, product, 0.0), axis=1, keepdims=True)
        base = 64 - base
        value = jnp.where(head_lanes, tiles[1] if head == 0 else tiles[2], place(lane, 64 if head == 0 else 0, (-1.0, -1.0, -1.0)))
        upstream = jnp.where(head_lanes, grad, place(lane, 64 if head == 0 else 0, split3(inner)))
        sides.append((slope, query.astype(BF), keys.astype(BF), value.astype(BF), upstream.astype(BF)))
    low_block = low[:size]
    for col_block in range(length // size):
        first = col_block if col_block * size >= PREFIX_MOST else 0
        cols = slice(col_block * size, (col_block + 1) * size)
        start = first * size
        results = []
        for head in range(2):
            slope, query, keys, value, upstream = sides[head]
            scores = dot(keys[cols], query[start:], NT)
            prob_grad = dot(value[cols], upstream[start:], NT)
            weights, score_grads = [], []
            for row_block in range(first, length // size):
                at = slice((row_block - first) * size, (row_block - first + 1) * size)
                piece = scores[:, at]
                if col_block >= row_block:
                    piece = piece + slope * masks[blocks.index((row_block, col_block))]
                powered = jnp.exp(piece)
                weights.append(powered.astype(BF))
                score_grads.append((powered * prob_grad[:, at]).astype(BF))
            weights = jnp.concatenate(weights, axis=1)
            score_grads = jnp.concatenate(score_grads, axis=1)
            value_grad = dot(weights, grad_low[start:], NN)
            key_grad = dot(score_grads, rolled_low[head][start:], NN) * 0.125
            query_grad = dot(score_grads, rolled_low[0 if head == 0 else 2][cols], TN)
            if col_block == 0:
                query_sum[head] = query_grad
            else:
                query_sum[head, start:] = query_sum[head, start:] + query_grad
            results.append((key_grad, value_grad))
        (key0, value0), (key1, value1) = results
        out_ref[cols, 0:128] = key0.astype(BF)
        out_ref[cols, 128:256] = value0.astype(BF)
        out_ref[cols, 256:384] = jnp.where(low_block, key1, value1).astype(BF)
    out_ref[:, 0:128] = jnp.where(low, query_sum[0] * 0.125, out_ref[:, 0:128].astype(F32)).astype(BF)
    out_ref[:, 128:256] = jnp.where(low, out_ref[:, 128:256].astype(F32), query_sum[1] * 0.125).astype(BF)
    half = length // 2
    chip = me_ref[0] >> 1
    final_ref[0:half, :] = out_ref[pl.ds(pl.multiple_of(chip * half, half), half), :]
    final_ref[half:, :] = out_ref[pl.ds(pl.multiple_of((1 - chip) * half, half), half), :]


def attend_backward(near, far, totals, context, grads, prefix, slopes, me, pair, size=256):
    length = 2 * near.shape[0]
    count = len(special_blocks(length, size))
    rows = grads[0].shape[0]
    tile = pl.BlockSpec((length, 128), lambda p, *_: (0, 0))
    return pl.pallas_call(
        partial(attend_backward_kernel, size),
        grid_spec=pltpu.PrefetchScalarGridSpec(
            num_scalar_prefetch=3,
            grid=(1,),
            in_specs=[pl.BlockSpec((length // 2, 384), lambda p, *_: (0, pair))] * 2
            + [tile, tile]
            + [pl.BlockSpec((rows, 128), lambda p, *_: (0, pair))] * 4,
            out_specs=pl.BlockSpec((length, 384), lambda p, *_: (0, 0)),
            scratch_shapes=[
                pltpu.VMEM((count, size, size), F32),
                pltpu.VMEM((2, length, 128), F32),
                pltpu.VMEM((length, 128), BF),
                pltpu.VMEM((length, 384), BF),
                pltpu.VMEM((length, 384), BF),
            ],
        ),
        out_shape=jax.ShapeDtypeStruct((length, 384), BF),
        compiler_params=pltpu.CompilerParams(vmem_limit_bytes=48 * 1024 * 1024),
        cost_estimate=pl.CostEstimate(flops=2 * 5 * 2 * length * length * 256, bytes_accessed=3 * 1024 * 1024, transcendentals=0),
        name="attend_backward",
    )(prefix, slopes[2 * pair : 2 * pair + 2], me, near, far, totals, context, *grads)


MIB = 1024 * 1024


def whole(shape):
    return pl.BlockSpec(shape, lambda *_: (0,) * len(shape))


def once(shape):
    return pl.BlockSpec(shape, lambda *_: (0,) * len(shape), pipeline_mode=pl.Buffered(1))


def project_kernel(me_ref, own_ref, near_ref, weight_ref, bias_ref, gain_ref, shift_ref, normed_ref, joined_ref):
    block = jnp.where(pl.program_id(0) == 0, own_ref[...].astype(F32), near_ref[...].astype(F32))
    normed = (norm_parts(block)[0] * gain_ref[...] + shift_ref[...]).astype(BF)
    normed_ref[...] = normed
    joined_ref[...] = (dot(normed, weight_ref[...], NN) + bias_ref[...]).astype(BF)


def project(me, blocks, weight, bias, gain, shift):
    rows, features = blocks[0].shape
    columns = weight.shape[1]
    return pl.pallas_call(
        project_kernel,
        grid_spec=pltpu.PrefetchScalarGridSpec(
            num_scalar_prefetch=1,
            grid=(2,),
            in_specs=[once((rows, features))] * 2
            + [once((features, columns)), once((1, columns)), once((1, features)), once((1, features))],
            out_specs=[
                pl.BlockSpec((rows, features), lambda g, me: ((me[0] & 1) ^ g, 0)),
                pl.BlockSpec((rows, columns), lambda g, me: ((me[0] & 1) ^ g, 0)),
            ],
        ),
        out_shape=[
            jax.ShapeDtypeStruct((2 * rows, features), BF),
            jax.ShapeDtypeStruct((2 * rows, columns), BF),
        ],
        compiler_params=pltpu.CompilerParams(vmem_limit_bytes=32 * 1024 * 1024),
        cost_estimate=pl.CostEstimate(flops=2 * 2 * rows * features * columns, bytes_accessed=6 * MIB, transcendentals=0),
        name="project",
    )(me, *blocks, weight, bias, gain, shift)


def middle_kernel(me_ref, *refs):
    (c0, c1, d0, d1, e0, e1, f0, f1, w0, w1, w2, w3, h0, h1, h2, h3, g0, g1, g2, g3, fc1_ref, fc2_ref, fc1_bias_ref,
     dense_bias_ref, gain_ref, shift_ref) = refs[:26]
    (normed_ref, act_ref, pre_ref, grad_ref, middle_ref, bias_sum_ref, squares_ref,
     part3_ref, part2_ref, part1_ref, part0_ref, hidden_ref) = refs[26:]
    step = pl.program_id(0)
    for at, (grad, hidden) in enumerate(((g3, h3), (g2, h2), (g1, h1), (g0, h0))):
        @pl.when(step == at)
        def _():
            grad_ref[...] = grad[...]
            hidden_ref[...] = hidden[...]
    grad = grad_ref[...]
    attn = dense_bias_ref[...]
    for halves, weight in (((c0, c1), w0), ((d0, d1), w1), ((e0, e1), w2), ((f0, f1), w3)):
        both = jnp.concatenate([half[...] for half in halves], axis=1)
        attn = attn + dot(both, weight[...], NN)
    middle = hidden_ref[...].astype(F32) + attn
    normed = (norm_parts(middle)[0] * gain_ref[...] + shift_ref[...]).astype(BF)
    normed_ref[...] = normed
    middle_ref[...] = middle
    squares_ref[...] = jnp.sum(attn * attn, axis=0, keepdims=True)
    pre = dot(normed, fc1_ref[...], NN) + fc1_bias_ref[...]
    act_grad = dot(grad, fc2_ref[...], NT)
    cubic = 0.7978845608028654
    square = pre * pre
    inner = jnp.tanh(pre * (cubic + cubic * 0.044715 * square))
    half = 0.5 + 0.5 * inner
    act = pre * half
    act_ref[...] = act.astype(BF)
    slope = half + act * (1.0 - inner) * (cubic + cubic * 3 * 0.044715 * square)
    pre_grad = (act_grad * slope).astype(BF)
    pre_ref[...] = pre_grad
    sums = jnp.sum(pre_grad.astype(F32), axis=0, keepdims=True)
    part = dot(pre_grad, fc1_ref[...], NT)

    @pl.when(step == 0)
    def _():
        bias_sum_ref[...] = sums

    @pl.when(step != 0)
    def _():
        bias_sum_ref[...] += sums

    for at, ref in enumerate((part3_ref, part2_ref, part1_ref, part0_ref)):
        @pl.when(step == at)
        def _():
            ref[...] = part.astype(ref.dtype)


def middle_part(me, contexts, weights, hidden, grads, fc1, fc2, fc1_bias, dense_bias, gain, shift):
    rows = hidden[0].shape[0]
    features, hidden_units = fc1.shape
    flip = lambda g, me: (3 - g, 0)
    placed = lambda g, me: (me[0] ^ (3 - g), 0)
    columns = contexts[0].shape[1]
    return pl.pallas_call(
        middle_kernel,
        grid_spec=pltpu.PrefetchScalarGridSpec(
            num_scalar_prefetch=1,
            grid=(4,),
            in_specs=[pl.BlockSpec((rows, columns), placed)] * 8
            + [once(w.shape) for w in weights]
            + [once((rows, features))] * 8
            + [once(fc1.shape), once(fc2.shape), once((1, hidden_units))] + [once((1, features))] * 3,
            out_specs=[
                pl.BlockSpec((rows, features), flip),
                pl.BlockSpec((rows, hidden_units), flip),
                pl.BlockSpec((rows, hidden_units), flip),
                pl.BlockSpec((rows, features), flip),
                whole((rows, features)),
                whole((1, hidden_units)),
                whole((1, features)),
            ]
            + [whole((rows, features))] * 4,
            scratch_shapes=[pltpu.VMEM((rows, features), BF)],
        ),
        out_shape=[
            jax.ShapeDtypeStruct((4 * rows, features), BF),
            jax.ShapeDtypeStruct((4 * rows, hidden_units), BF),
            jax.ShapeDtypeStruct((4 * rows, hidden_units), BF),
            jax.ShapeDtypeStruct((4 * rows, features), BF),
            jax.ShapeDtypeStruct((rows, features), F32),
            jax.ShapeDtypeStruct((1, hidden_units), F32),
            jax.ShapeDtypeStruct((1, features), F32),
        ]
        + [jax.ShapeDtypeStruct((rows, features), kind) for kind in (BF, F32, BF, F32)],
        compiler_params=pltpu.CompilerParams(vmem_limit_bytes=56 * 1024 * 1024),
        cost_estimate=pl.CostEstimate(flops=2 * 4 * rows * features * (features + 3 * hidden_units), bytes_accessed=14 * MIB, transcendentals=0),
        name="middle_part",
    )(me, *contexts, *weights, *hidden, *grads, fc1, fc2, fc1_bias, dense_bias, gain, shift)


def turn_kernel(part_ref, near_ref, far_ref, middle_ref, out_grad_ref, gain_ref, w0, w1, w2, w3,
                grad_ref, low_ref, g0, g1, g2, g3, sums_ref):
    upstream = part_ref[...] + near_ref[...].astype(F32) + far_ref[...].astype(F32)
    unit, rstd = norm_parts(middle_ref[...])
    scaled = upstream * gain_ref[...]
    grad = rstd * (
        scaled
        - jnp.mean(scaled, axis=-1, keepdims=True)
        - unit * jnp.mean(scaled * unit, axis=-1, keepdims=True)
    )
    out_grad = out_grad_ref[...].astype(F32)
    grad = grad + out_grad
    low = grad.astype(BF)
    grad_ref[...] = grad
    low_ref[...] = low
    for weight, ref in ((w0, g0), (w1, g1), (w2, g2), (w3, g3)):
        ref[...] = dot(low, weight[...], NT).astype(BF)
    sums_ref[0:1, :] = jnp.sum(grad, axis=0, keepdims=True)
    sums_ref[1:2, :] = jnp.sum(upstream * unit, axis=0, keepdims=True)
    sums_ref[2:3, :] = jnp.sum(upstream, axis=0, keepdims=True)
    sums_ref[3:4, :] = jnp.sum(out_grad, axis=0, keepdims=True)
    sums_ref[4:8, :] = jnp.zeros((4, grad.shape[1]), F32)


def turn(part, near, far, middle, out_grad, gain, weights):
    rows, features = middle.shape
    heads = weights[0].shape[0]
    return pl.pallas_call(
        turn_kernel,
        out_shape=[
            jax.ShapeDtypeStruct((rows, features), F32),
            jax.ShapeDtypeStruct((rows, features), BF),
        ]
        + [jax.ShapeDtypeStruct((rows, heads), BF)] * 4
        + [jax.ShapeDtypeStruct((8, features), F32)],
        compiler_params=pltpu.CompilerParams(vmem_limit_bytes=32 * 1024 * 1024),
        cost_estimate=pl.CostEstimate(flops=2 * 4 * rows * features * heads, bytes_accessed=7 * MIB, transcendentals=0),
        name="turn",
    )(part, near, far, middle, out_grad, gain, *weights)


def first_part_kernel(me_ref, grad_ref, weight_ref, part3_ref, part2_ref, part1_ref, part0_ref):
    step = pl.program_id(0)
    part = dot(grad_ref[...], weight_ref[...], NT)
    for at, ref in enumerate((part3_ref, part2_ref, part1_ref, part0_ref)):
        @pl.when(step == at)
        def _():
            ref[...] = part.astype(ref.dtype)


def first_part(me, grad, weight):
    rows, features = grad.shape[0] // 4, weight.shape[0]
    return pl.pallas_call(
        first_part_kernel,
        grid_spec=pltpu.PrefetchScalarGridSpec(
            num_scalar_prefetch=1,
            grid=(4,),
            in_specs=[pl.BlockSpec((rows, grad.shape[1]), lambda g, me: ((me[0] & 1) ^ (3 - g), 0)), once(weight.shape)],
            out_specs=[whole((rows, features))] * 4,
        ),
        out_shape=[jax.ShapeDtypeStruct((rows, features), kind) for kind in (BF, F32, BF, F32)],
        compiler_params=pltpu.CompilerParams(vmem_limit_bytes=32 * 1024 * 1024),
        cost_estimate=pl.CostEstimate(flops=2 * 4 * rows * features * grad.shape[1], bytes_accessed=6 * MIB, transcendentals=0),
        name="first_part",
    )(me, grad, weight)


def last_kernel(part_ref, near_ref, far_ref, hidden_ref, middle_grad_ref, gain_ref, out_ref, sums_ref):
    upstream = part_ref[...] + near_ref[...].astype(F32) + far_ref[...].astype(F32)
    unit, rstd = norm_parts(hidden_ref[...].astype(F32))
    scaled = upstream * gain_ref[...]
    grad = rstd * (
        scaled
        - jnp.mean(scaled, axis=-1, keepdims=True)
        - unit * jnp.mean(scaled * unit, axis=-1, keepdims=True)
    )
    out_ref[...] = (grad + middle_grad_ref[...]).astype(BF)
    sums_ref[0:1, :] = jnp.sum(upstream * unit, axis=0, keepdims=True)
    sums_ref[1:2, :] = jnp.sum(upstream, axis=0, keepdims=True)
    sums_ref[2:8, :] = jnp.zeros((6, grad.shape[1]), F32)


def last_norm(part, near, far, hidden, middle_grad, gain):
    rows, features = hidden.shape
    return pl.pallas_call(
        last_kernel,
        out_shape=[jax.ShapeDtypeStruct((rows, features), BF), jax.ShapeDtypeStruct((8, features), F32)],
        compiler_params=pltpu.CompilerParams(vmem_limit_bytes=32 * 1024 * 1024),
        cost_estimate=pl.CostEstimate(flops=2 * rows * features * 16, bytes_accessed=5 * MIB, transcendentals=0),
        name="last_norm",
    )(part, near, far, hidden, middle_grad, gain)


def tensor_send(value, flip):
    return lax.ppermute(value, "tensor", [(i, i ^ flip) for i in range(4)])


def add_low(a, b):
    return (a.astype(F32) + b.astype(F32)).astype(BF)


class Ladder:
    def __init__(self, dp, array):
        self.inner, self.outer = 2, dp // 2
        index = lax.axis_index("dp")
        self.mine, self.place_of = index % 2, index // 2
        self.pairs = [(i, i ^ 1) for i in range(dp)]
        self.array, self.half = array, array.shape[0] // 2
        half = self.outer // 2
        count = self.outer
        self.steps = [("in", s) for s in range(half - 1)] + ([("mid", 0)] if count > 1 else [])
        self.steps += [("out", s) for s in reversed(range(half - 1))]
        self.stages = len(self.steps) + 2
        self.stage = 0
        self.came = self.value = None
        self.open = False

    def along(self, pairs):
        return [(a * self.inner + i, b * self.inner + i) for a, b in pairs for i in range(self.inner)]

    def part(self, which):
        return lax.dynamic_slice_in_dim(self.array, which * self.half, self.half, 0)

    def send(self, *gate):
        count, half = self.outer, self.outer // 2
        if self.stage == 0:
            self.sent, pairs = self.part(1 - self.mine), self.pairs
        elif self.stage == self.stages - 1:
            self.sent, pairs = self.value, self.pairs
        else:
            kind, step = self.steps[self.stage - 1]
            self.sent = self.value
            if kind == "in":
                pairs = [(step, step + 1), (count - 1 - step, count - 2 - step)]
            elif kind == "mid":
                pairs = [(half - 1, half), (half, half - 1)]
            else:
                pairs = [(step + 1, step), (count - 2 - step, count - 1 - step)]
            pairs = self.along(pairs)
        if gate:
            self.sent = after(self.sent, *gate)
        self.came = lax.ppermute(self.sent, "dp", pairs)
        self.open = True
        return self

    def take(self, *gate):
        count = self.outer
        if gate and self.value is not None:
            self.value = after(self.value, *gate)
        if self.stage == 0:
            own = self.part(self.mine)
            if gate:
                own = after(own, *gate)
            self.value = add_low(own, self.came)
        elif self.stage < self.stages - 1:
            kind, step = self.steps[self.stage - 1]
            if kind == "out":
                outside = (self.place_of <= step) | (self.place_of >= count - 1 - step)
                self.value = jnp.where(outside, self.came, self.value)
            else:
                self.value = add_low(self.value, self.came)
        self.stage += 1
        self.open = False
        return self

    def finish(self):
        if self.came is not None and self.open:
            self.take()
        while self.stage < self.stages:
            self.send().take()
        return self

    def rows(self):
        lower = self.mine == 0
        return [jnp.where(lower, self.value, self.came), jnp.where(lower, self.came, self.value)]


class Spread:
    def __init__(self, dp, array):
        self.lines = [[a * 2 + i for a in range(dp // 2)] for i in range(2)]
        self.pairs = [(i, i ^ 1) for i in range(dp)]
        self.mine = lax.axis_index("dp") % 2
        self.array = array
        self.blocks = array.reshape(dp // 2, 2, array.shape[0] // dp, array.shape[1])

    def send(self):
        self.came = lax.ppermute(lax.dynamic_index_in_dim(self.blocks, 1 - self.mine, 1, False), "dp", self.pairs)

    def take(self, *gate):
        self.value = add_low(after(lax.dynamic_index_in_dim(self.blocks, self.mine, 1, False), *gate), self.came)
        return self

    def trade(self):
        self.terms = lax.all_to_all(self.value, "dp", 0, 0, axis_index_groups=self.lines, tiled=True)

    def add(self, *gate):
        self.value = jnp.sum(after(self.terms, *gate).astype(F32), axis=0).astype(BF)
        return self

    def gather(self):
        self.all = lax.all_gather(self.value, "dp", axis=0, tiled=True)


def joined_rows(ladders):
    return jnp.concatenate([piece for ladder in ladders for piece in ladder.rows()], axis=0).astype(F32)


def small_sum(value, dp, axes):
    if "dp" in axes:
        step = 1
        while step < dp:
            value = value + lax.ppermute(value, "dp", [(i, i ^ step) for i in range(dp)])
            step *= 2
    if "tensor" in axes:
        for step in (1, 2):
            value = value + tensor_send(value, step)
    return value


def local(
    dp,
    hidden_in,
    out_grad,
    prefix_len,
    qkv_weight,
    qv_bias,
    dense_weight,
    dense_bias,
    norm1_gain,
    norm1_shift,
    norm2_gain,
    norm2_shift,
    fc1_weight,
    fc1_bias,
    fc2_weight,
    fc2_bias,
):
    rows_here, features = hidden_in.shape
    heads_here, _, head_size = qv_bias.shape
    tensor_index = lax.axis_index("tensor")
    me = tensor_index.reshape(1)
    slopes = 2.0 ** (-8.0 * (tensor_index * heads_here + 1 + lax.iota(jnp.int32, heads_here)).astype(F32) / HEADS)
    bias_full = jnp.stack(
        [qv_bias[:, 0], jnp.zeros_like(qv_bias[:, 0]), qv_bias[:, 1]], axis=1
    ).reshape(1, -1)
    row = lambda v: v.reshape(1, -1)

    norm1 = (qkv_weight, bias_full, row(norm1_gain), row(norm1_shift))
    hidden_x = tensor_send(hidden_in, 2)
    hidden_c = tensor_send(hidden_in, 1)
    dense_c = tensor_send(dense_weight, 1)
    normed_near, joined_near = project(me, (hidden_in, hidden_c), *norm1)
    share = dense_weight.shape[0] // 2
    parity = lax.axis_index("dp") % 2
    dense_share = lax.dynamic_slice_in_dim(dense_weight, parity * share, share, 0)
    hidden_xc = tensor_send(after(hidden_x, joined_near), 1)
    dense_half = tensor_send(after(dense_share, hidden_x, joined_near), 2)
    normed_far, joined_far = project(me, (hidden_x, hidden_xc), *norm1)
    grad_c = tensor_send(after(out_grad, hidden_c), 1)
    context0, totals0 = attend_forward(joined_near, joined_far, prefix_len, slopes, me, 0)
    context0_x = tensor_send(context0, 2)
    context0_c = tensor_send(context0, 1)
    grad_x = tensor_send(after(out_grad, dense_half, context0), 2)
    dense_other = lax.ppermute(after(dense_half, context0), "dp", [(i, i ^ 1) for i in range(dp)])
    context1, totals1 = attend_forward(after(joined_near, context0_c), joined_far, prefix_len, slopes, me, 1)
    context1_x = tensor_send(context1, 2)
    context1_c = tensor_send(context1, 1)
    dense_x = jnp.where(
        parity == 0,
        jnp.concatenate([dense_half, dense_other], axis=0),
        jnp.concatenate([dense_other, dense_half], axis=0),
    )
    dense_xc = tensor_send(dense_x, 1)
    dense_blocks = [dense_weight, dense_c, dense_x, dense_xc]
    grad_xc = tensor_send(grad_x, 1)
    context0_xc = tensor_send(context0_x, 1)
    context1_xc = tensor_send(context1_x, 1)

    contexts = [context0, context1, context0_c, context1_c, context0_x, context1_x, context0_xc, context1_xc]
    (normed2_all, activated, pre_grad, grad_all, middle, fc1_bias_sum, attn_squares, part3, part2, part1, part0) = middle_part(
        me, contexts, dense_blocks, (hidden_in, hidden_c, hidden_x, hidden_xc), (out_grad, grad_c, grad_x, grad_xc),
        fc1_weight, fc2_weight, row(fc1_bias), row(dense_bias), row(norm2_gain), row(norm2_shift),
    )

    over = tensor_send(part3, 1)
    near = tensor_send(part1, 1)
    half = features // 2
    fc1_term = dot(normed2_all, pre_grad, TN).astype(BF)
    b1, b2 = Ladder(dp, fc1_term[:half]), Ladder(dp, fc1_term[half:])
    b1.send()
    chip = (after(part2, b1.sent) + over.astype(F32)).astype(BF)
    far = tensor_send(chip, 2)
    fc2_term = dot(after(activated, chip), grad_all, TN).astype(BF)
    a1, a2 = Ladder(dp, fc2_term[:half]), Ladder(dp, fc2_term[half:])
    b2.send(fc2_term)
    b1.take(b2.sent).send()
    middle_grad, middle_low, *context_grads, turn_sums = turn(
        after(part0, b1.value), near, far, middle, out_grad, row(norm2_gain), dense_blocks
    )
    arrived = [context_grads[0]] + [tensor_send(context_grads[flip], flip) for flip in (2, 3, 1)]
    arrived = [arrived[0], arrived[3], arrived[1], arrived[2]]
    b1.take(middle_low).send()
    b2.take(b1.value).send()
    joined_grad0 = attend_backward(
        after(joined_near, b2.value), joined_far, totals0, context0, arrived, prefix_len, slopes, me, 0
    )
    a1.send(joined_grad0)
    middle_x = tensor_send(after(middle_low, joined_grad0), 2)
    normed1_all = jnp.concatenate([after(normed_near, joined_grad0), normed_far], axis=0)
    b1.take(a1.sent).send()
    b2.take(b1.value).send()
    middle_c = tensor_send(after(middle_low, b2.value), 1)
    joined_grad1 = attend_backward(
        after(joined_near, b2.value, normed1_all), joined_far, totals1, context1, arrived, prefix_len, slopes, me, 1
    )
    a1.take(joined_grad1).send()
    a2.send(a1.value)
    middle_xc = tensor_send(after(middle_x, joined_grad1), 1)
    c1 = Ladder(dp, dot(after(normed1_all, a2.sent), joined_grad0, TN).astype(BF))
    b1.take(c1.array).send()
    b2.take(b1.value).send()
    a1.take(b2.value).send()
    a2.take(a1.value).send()
    c1.send(a2.value)
    qkv_term = dot(after(normed1_all, c1.sent), joined_grad1, TN).astype(BF)
    middle_all = jnp.concatenate([after(middle_low, c1.sent), middle_c, middle_x, middle_xc], axis=0)
    context = jnp.concatenate([context0, context1], axis=1)
    context_flip = jnp.concatenate(
        [lax.dynamic_slice_in_dim(context, (tensor_index ^ flip) * rows_here, rows_here, 0) for flip in range(4)], axis=0
    )
    dense_term = dot(after(middle_all, qkv_term), context_flip, TN).astype(BF)
    c2 = Ladder(dp, jnp.concatenate([qkv_term, dense_term], axis=1))
    b1.take(c2.array)
    b2.take(b1.value).send()
    a1.take(b2.value).send()
    a2.take(a1.value).send()
    c1.take(a2.value).send()
    c2.send(c1.value)
    joined_grad = jnp.concatenate([joined_grad0, joined_grad1], axis=1)
    last3, last2, last1, last0 = first_part(me, after(joined_grad, c2.sent), qkv_weight)
    b2.take(last0)
    a1.take(b2.value).send()
    a2.take(a1.value).send()
    c1.take(a2.value).send()
    c2.take(c1.value).send()
    last_over = tensor_send(after(last3, c2.value), 1)
    last_near = tensor_send(after(last1, c2.value), 1)
    late = after(activated, c2.value)
    mlp3, mlp2, mlp1, mlp0 = (
        dot(late[flip * rows_here : (flip + 1) * rows_here], fc2_weight, NN) for flip in (3, 2, 1, 0)
    )
    last_chip = (after(last2, mlp0) + last_over.astype(F32)).astype(BF)
    last_far = tensor_send(last_chip, 2)
    a1.take(last_chip)
    a2.take(a1.value).send()
    c1.take(a2.value).send()
    c2.take(c1.value).send()
    mlp_over = tensor_send(after(mlp3, c2.value).astype(BF), 1)
    mlp_near = tensor_send(after(mlp1, c2.value).astype(BF), 1)
    fc1_sum = joined_rows([b1, b2])
    hidden_grad, last_sums = last_norm(
        after(last0, c2.value), last_near, last_far, hidden_in, middle_grad, row(norm1_gain)
    )
    mlp_chip = (after(mlp2, hidden_grad) + mlp_over.astype(F32)).astype(BF)
    mlp_far = tensor_send(mlp_chip, 2)
    a2.take(mlp_chip)
    c1.take(a2.value).send()
    c2.take(c1.value).send()
    fc2_sum = joined_rows([a1, a2])
    mlp_out = after(mlp0, c2.value) + mlp_near.astype(F32) + mlp_far.astype(F32) + fc2_bias
    final = middle + mlp_out
    residual = hidden_in.astype(F32)
    c1.take(final)
    c2.take(c1.value).send()
    last_sums = after(last_sums, c2.value)
    c2.finish()
    last_sum = joined_rows([c2])

    joined_sums = jnp.sum(joined_grad.astype(F32), axis=0).reshape(heads_here, 3, head_size)
    qv_sums = jnp.stack([joined_sums[:, 0], joined_sums[:, 2]], axis=1).reshape(1, -1)
    squares = jnp.stack(
        [jnp.sum(residual * residual), jnp.sum(attn_squares), jnp.sum(mlp_out * mlp_out), jnp.sum(final * final)]
    ).reshape(1, -1)
    widen = lambda v: jnp.pad(v, ((0, 0), (0, features - v.shape[1])))
    by_dp = small_sum(
        jnp.concatenate(
            [fc1_bias_sum, widen(qv_sums), widen(squares), turn_sums[:4], last_sums[:2]], axis=0
        ),
        dp,
        ("dp",),
    )
    by_all = small_sum(by_dp[2:], dp, ("tensor",))
    qv_bias_grad = by_dp[1, : qv_sums.shape[1]].reshape(heads_here, 2, head_size)
    entry_count = rows_here * features * dp * 4
    sublayer_rms = jnp.sqrt(by_all[0, :4] / float(entry_count))
    return (
        final.astype(BF),
        hidden_grad,
        jnp.concatenate([joined_rows([c1]), last_sum[:, : qkv_term.shape[1]]], axis=1),
        qv_bias_grad,
        last_sum[:, qkv_term.shape[1] :].T,
        by_all[1],
        by_all[5],
        by_all[6],
        by_all[2],
        by_all[3],
        fc1_sum.astype(F32),
        by_dp[0],
        fc2_sum.astype(F32),
        by_all[4],
        sublayer_rms,
    )


def solution(mesh):
    return jax.shard_map(
        partial(local, mesh.shape["dp"]),
        mesh=mesh,
        in_specs=(
            P(("dp", "tensor"), None),
            P(("dp", "tensor"), None),
            P("dp"),
            P(None, "tensor"),
            P("tensor", None, None),
            P("tensor", None),
            P(),
            P(),
            P(),
            P(),
            P(),
            P(None, "tensor"),
            P("tensor"),
            P("tensor", None),
            P(),
        ),
        out_specs=(
            P(("dp", "tensor"), None),
            P(("dp", "tensor"), None),
            P(None, "tensor"),
            P("tensor", None, None),
            P("tensor", None),
            P(),
            P(),
            P(),
            P(),
            P(),
            P(None, "tensor"),
            P("tensor"),
            P("tensor", None),
            P(),
            P(),
        ),
        check_vma=False,
    )
```

time: 508 us -> 327 us (0.64); the launches traced: 499 us -> 324 us
  waiting for transfers between devices: 220 us -> 112 us
  starting transfers between devices: 124 us -> 75.1 us
  matrix products: 55.9 us -> 13.2 us
  Pallas kernels: 20.5 us -> 62.8 us
  other arithmetic: 43.3 us -> 31.8 us
    ppermute x65 -> x31, waiting for transfers between devices: 189 us -> 75.5 us  [the longest x30 75.5 us: send(): self.came = lax.ppermute(self.sent, 'dp', pairs)]
    ppermute x65 -> x31, starting transfers between devices: 103 us -> 55.5 us  [the longest x30 54 us: send(): self.came = lax.ppermute(self.sent, 'dp', pairs)]
    dot_general x46 -> x9, matrix products: 55.9 us -> 13.2 us  [dot(): return lax.dot_general(a, b, dims, preferred_element_type=F32)]
    pallas_call x0 -> x6, Pallas kernels: none -> 42.2 us  [the longest x1 32.5 us: middle_part(): pl.pallas_call(middle_kernel, grid_spec=pltpu.PrefetchScalarGridSpec(num_...]
    dynamic_update_slice x15 -> x0, local copies, waits for them, and re-layouts: 12 us -> none  [in_order(): out = lax.dynamic_update_slice_in_dim(out, block, (me ^ flip) * rows, 0)]
    unnamed x21 -> x0, other arithmetic: 8 us -> none
    reduce_sum x10 -> x3, other arithmetic: 9.59 us -> 3.27 us  [the longest x1 1.79 us: local(): jnp.sum(final * final)]
    convert_element_type x26 -> x18, other arithmetic: 2.66 us -> 7.86 us  [add_low(): return (a.astype(F32) + b.astype(F32)).astype(BF)]
  transfers between devices with their start and end apart: 97 -> 66, of which waited for: 46 -> 24; matrix products, arithmetic and copies ran while one was open for 21% -> 16% of each run, Pallas kernels for 4% -> 9%
where the time goes in v2:
time: 327 us; the launch traced here: 324 us
  waiting for transfers between devices  112 us (34%)
  starting transfers between devices  75.1 us (23%)
  Pallas kernels  62.8 us (19%)
  other arithmetic  31.8 us (10%)
  local copies, waits for them, and re-layouts  26.7 us (8%)
  matrix products  13.2 us (4%)
    ppermute x30, waiting for transfers between devices, send(): self.came = lax.ppermute(self.sent, 'dp', pairs)  75.5 us
    ppermute x30, starting transfers between devices, send(): self.came = lax.ppermute(self.sent, 'dp', pairs)  54 us
    pallas_call x1, Pallas kernels, middle_part(): pl.pallas_call(middle_kernel, grid_spec=pltpu.PrefetchScalarGridSpec(num_...  32.5 us
    ppermute x32, waiting for transfers between devices, tensor_send(): return lax.ppermute(value, 'tensor', [(i, i ^ flip) for i in range(4)])  27.5 us
    unnamed x133, local copies, waits for them, and re-layouts  17.7 us
    ppermute x32, starting transfers between devices, tensor_send(): return lax.ppermute(value, 'tensor', [(i, i ^ flip) for i in range(4)])  17.6 us
    dot_general x9, matrix products, dot(): return lax.dot_general(a, b, dims, preferred_element_type=F32)  13.2 us
    pallas_call x2, Pallas kernels, attend_backward(): pl.pallas_call(partial(attend_backward_kernel, size), grid_spec=pltpu.Pre...  12.1 us
  transfers between devices with their start and end apart: 66, of which 24 were waited for; matrix products, arithmetic and copies ran while one was open for 16% of the time, Pallas kernels for 9%

profile of v2, /device:TPU:0, one launch (start us, length us, event | category | flops | bytes accessed | tf_op | source)
XLA Modules:
  0.0 324.2 jit_solution(13296862529538576527)
XLA Ops:
  1.2 2.6 collective-permute-start.1
  11.6 4.9 %collective-permute-done.1.own_ref.refs_14_ = bf16[256,1024]{1,0:T(8,128)(2,1)S(1)} collective-permute-done((bf16[256,1024]{1,0:T(8,128)(2,1)}, bf16[256,1024]{1,0:T(8,128)(2,1)S(1)}, u32[]{:S(2)}, u32[]{:S(2)}) %collective-permute-start.1) | collective-permute-done | bytes 524320 | tf_op jit(solution)/shard_map/ppermute | solution.py:507
  24.7 4.3 %attend_forward.2 = (bf16[1024,128]{1,0:T(8,128)(2,1)S(1)}, f32[1024,128]{1,0:T(8,128)S(1)}) custom-call(s32[1]{0:T(128)S(6)} %copy.40.prefix_ref, f32[2]{0:T(128)S(1)} %get-tuple-element.283.slope_ref, s32[1]{0:T(128)} %bitcast.me_ref, bf16[512,768]{1,0:T(8,128)(2,1)S(1)} %get-tuple-element.150.near_ref, bf16[512,768]{1,0:T(8,128)(2,1)S(1)} %get-tuple-element.113.far_ref), custom_call_target="tpu_custom_call" | custom-call | flops 1073741824 | bytes 2097152 | tf_op jit(solution)/shard_map/attend_forward/pallas_call | solution.py:148
  35.9 4.3 %attend_forward.3 = (bf16[1024,128]{1,0:T(8,128)(2,1)S(1)}, f32[1024,128]{1,0:T(8,128)S(1)}) custom-call(s32[1]{0:T(128)S(6)} %copy.40.prefix_ref, f32[2]{0:T(128)S(1)} %get-tuple-element.282.slope_ref, s32[1]{0:T(128)} %bitcast.me_ref, bf16[512,768]{1,0:T(8,128)(2,1)S(1)} %copy-done.37, bf16[512,768]{1,0:T(8,128)(2,1)S(1)} %copy-done.40), custom_call_target="tpu_custom_call" | custom-call | flops 1073741824 | bytes 2097152 | tf_op jit(solution)/shard_map/attend_forward/pallas_call | solution.py:148
  46.2 4.2 %collective-permute-done.5.refs_4_ = bf16[1024,128]{1,0:T(8,128)(2,1)} collective-permute-done((bf16[1024,128]{1,0:T(8,128)(2,1)S(1)}, bf16[1024,128]{1,0:T(8,128)(2,1)}, u32[]{:S(2)}, u32[]{:S(2)}) %collective-permute-start.5) | collective-permute-done | bytes 262176 | tf_op jit(solution)/shard_map/ppermute | solution.py:507
  50.4 4.4 %collective-permute-done.6.refs_5_ = bf16[1024,128]{1,0:T(8,128)(2,1)} collective-permute-done((bf16[1024,128]{1,0:T(8,128)(2,1)S(1)}, bf16[1024,128]{1,0:T(8,128)(2,1)}, u32[]{:S(2)}, u32[]{:S(2)}) %collective-permute-start.6) | collective-permute-done | bytes 262176 | tf_op jit(solution)/shard_map/ppermute | solution.py:507
  57.3 32.5 %middle_part.1 = (bf16[1024,1024]{1,0:T(8,128)(2,1)}, bf16[1024,1024]{1,0:T(8,128)(2,1)}, bf16[1024,1024]{1,0:T(8,128)(2,1)}, bf16[1024,1024]{1,0:T(8,128)(2,1)}...) custom-call(s32[1]{0:T(128)} %bitcast.me_ref, ...), custom_call_target="tpu_custom_call" | custom-call | flops 8589934592 | bytes 14680064 | tf_op jit(solution)/shard_map/middle_part/pallas_call | solution.py:376
  89.9 4.6 %convolution_convert_fusion.1 = bf16[1024,1024]{1,0:T(8,128)(2,1)S(1)} fusion(bf16[1024,1024]{1,0:T(8,128)(2,1)} %get-tuple-element.124, bf16[1024,1024]{1,0:T(8,128)(2,1)} %get-tuple-element.125), kind=kOutput, calls=%fused_computation.6 | convolution fusion | flops 2148532224 | bytes 6291456 | tf_op jit(solution)/shard_map/dot_general | solution.py:22
  103.3 7.4 %collective-permute-done.17 = bf16[256,1024]{1,0:T(8,128)(2,1)} collective-permute-done((bf16[256,1024]{1,0:T(8,128)(2,1)}, bf16[256,1024]{1,0:T(8,128)(2,1)}, u32[]{:S(2)}, u32[]{:S(2)}) %collective-permute-start.17) | collective-permute-done | bytes 524320 | tf_op jit(solution)/shard_map/ppermute | solution.py:554
  111.9 3.5 %collective-permute-start.20 = (bf16[256,1024]{1,0:T(8,128)(2,1)S(1)}, bf16[256,1024]{1,0:T(8,128)(2,1)S(1)}, u32[]{:S(2)}, u32[]{:S(2)}) collective-permute-start(bf16[256,1024]{1,0:T(8,128)(2,1)S(1)} %add_convert_fusion.16), channel_id=1, source_target_pairs={{0,8},{4,12},{24,16},{28,20},{1,9},{5,13},{25,17},{29,21},{2,10},{... | collective-permute-start | bytes 1572872 | tf_op jit(solution)/shard_map/ppermute | solution.py:554
  120.2 5.5 %collective-permute-done.20 = bf16[256,1024]{1,0:T(8,128)(2,1)S(1)} collective-permute-done((bf16[256,1024]{1,0:T(8,128)(2,1)S(1)}, bf16[256,1024]{1,0:T(8,128)(2,1)S(1)}, u32[]{:S(2)}, u32[]{:S(2)}) %collective-permute-start.20) | collective-permute-done | bytes 524320 | tf_op jit(solution)/shard_map/ppermute | solution.py:554
  128.7 7.2 %collective-permute-start.26 = (bf16[256,1024]{1,0:T(8,128)(2,1)S(1)}, bf16[256,1024]{1,0:T(8,128)(2,1)S(1)}, u32[]{:S(2)}, u32[]{:S(2)}) collective-permute-start(bf16[256,1024]{1,0:T(8,128)(2,1)S(1)} %add_convert_fusion.14), channel_id=1, source_target_pairs={{0,8},{4,12},{24,16},{28,20},{1,9},{5,13},{25,17},{29,21},{2,10},{... | collective-permute-start | bytes 1572872 | tf_op jit(solution)/shard_map/ppermute | solution.py:554
  136.6 6.0 %attend_backward.2 = bf16[1024,384]{1,0:T(8,128)(2,1)S(1)} custom-call(s32[1]{0:T(128)S(6)} %copy.40.prefix_ref, f32[2]{0:T(128)S(1)} %get-tuple-element.283.slope_ref, s32[1]{0:T(128)} %bitcast.me_ref, bf16[512,768]{1,0:T(8,128)(2,1)S(1)} %copy-done.38, bf16[512,768]{1,0:T(8,128)(2,1)S(1)} %copy-done.41, f32[1024,128]{1,0:T(8,128)S(1)} %copy-done.45, ...), custom_call_target="tpu_custom_call" | custom-call | flops 5368709120 | bytes 3145728 | tf_op jit(solution)/shard_map/attend_backward/pallas_call | solution.py:254
  150.5 6.0 %attend_backward.3 = bf16[1024,384]{1,0:T(8,128)(2,1)S(1)} custom-call(s32[1]{0:T(128)S(6)} %copy.40.prefix_ref, f32[2]{0:T(128)S(1)} %get-tuple-element.282.slope_ref, s32[1]{0:T(128)} %bitcast.me_ref, bf16[512,768]{1,0:T(8,128)(2,1)S(1)} %copy-done.38, bf16[512,768]{1,0:T(8,128)(2,1)S(1)} %copy-done.41, f32[1024,128]{1,0:T(8,128)S(1)} %copy-done.43, ...), custom_call_target="tpu_custom_call" | custom-call | flops 5368709120 | bytes 3145728 | tf_op jit(solution)/shard_map/attend_backward/pallas_call | solution.py:254
  159.4 7.2 %collective-permute-start.30 = (bf16[256,1024]{1,0:T(8,128)(2,1)S(1)}, bf16[256,1024]{1,0:T(8,128)(2,1)S(1)}, u32[]{:S(2)}, u32[]{:S(2)}) collective-permute-start(bf16[256,1024]{1,0:T(8,128)(2,1)S(1)} %add_convert_fusion.11), channel_id=1, source_target_pairs={{0,8},{4,12},{24,16},{28,20},{1,9},{5,13},{25,17},{29,21},{2,10},{... | collective-permute-start | bytes 1572872 | tf_op jit(solution)/shard_map/ppermute | solution.py:554
  172.6 5.8 %collective-permute-done.30 = bf16[256,1024]{1,0:T(8,128)(2,1)S(1)} collective-permute-done((bf16[256,1024]{1,0:T(8,128)(2,1)S(1)}, bf16[256,1024]{1,0:T(8,128)(2,1)S(1)}, u32[]{:S(2)}, u32[]{:S(2)}) %collective-permute-start.30) | collective-permute-done | bytes 524320 | tf_op jit(solution)/shard_map/ppermute | solution.py:554
  179.1 3.7 %collective-permute-done.31 = bf16[256,1024]{1,0:T(8,128)(2,1)S(1)} collective-permute-done((bf16[256,1024]{1,0:T(8,128)(2,1)S(1)}, bf16[256,1024]{1,0:T(8,128)(2,1)S(1)}, u32[]{:S(2)}, u32[]{:S(2)}) %collective-permute-start.31) | collective-permute-done | bytes 524320 | tf_op jit(solution)/shard_map/ppermute | solution.py:554
  185.0 3.8 %collective-permute-start.37 = (bf16[256,1024]{1,0:T(8,128)(2,1)S(1)}, bf16[256,1024]{1,0:T(8,128)(2,1)S(1)}, u32[]{:S(2)}, u32[]{:S(2)}) collective-permute-start(bf16[256,1024]{1,0:T(8,128)(2,1)S(1)} %add_convert_fusion.8), channel_id=1, source_target_pairs={{0,8},{4,12},{24,16},{28,20},{1,9},{5,13},{25,17},{29,21},{2,10},{... | collective-permute-start | bytes 1572872 | tf_op jit(solution)/shard_map/ppermute | solution.py:554
  195.8 3.7 %collective-permute-done.37 = bf16[256,1024]{1,0:T(8,128)(2,1)S(1)} collective-permute-done((bf16[256,1024]{1,0:T(8,128)(2,1)S(1)}, bf16[256,1024]{1,0:T(8,128)(2,1)S(1)}, u32[]{:S(2)}, u32[]{:S(2)}) %collective-permute-start.37) | collective-permute-done | bytes 524320 | tf_op jit(solution)/shard_map/ppermute | solution.py:554
  202.5 4.3 %collective-permute-start.41 = (bf16[512,384]{1,0:T(8,128)(2,1)S(1)}, bf16[512,384]{1,0:T(8,128)(2,1)S(1)}, u32[]{:S(2)}, u32[]{:S(2)}) collective-permute-start(bf16[512,384]{1,0:T(8,128)(2,1)S(1)} %add_convert_fusion.20), channel_id=1, source_target_pairs={{0,8},{4,12},{24,16},{28,20},{1,9},{5,13},{25,17},{29,21},{2,10},{... | collective-permute-start | bytes 1179656 | tf_op jit(solution)/shard_map/ppermute | solution.py:554
  208.0 2.7 first_part.1
  210.7 2.9 collective-permute-done.63
  218.9 8.1 %collective-permute-done.42 = bf16[512,640]{1,0:T(8,128)(2,1)S(1)} collective-permute-done((bf16[512,640]{1,0:T(8,128)(2,1)S(1)}, bf16[512,640]{1,0:T(8,128)(2,1)S(1)}, u32[]{:S(2)}, u32[]{:S(2)}) %collective-permute-start.42) | collective-permute-done | bytes 655392 | tf_op jit(solution)/shard_map/ppermute | solution.py:554
  227.2 3.1 collective-permute-start.46
  233.9 9.3 %collective-permute-done.46 = bf16[512,640]{1,0:T(8,128)(2,1)S(1)} collective-permute-done((bf16[512,640]{1,0:T(8,128)(2,1)S(1)}, bf16[512,640]{1,0:T(8,128)(2,1)S(1)}, u32[]{:S(2)}, u32[]{:S(2)}) %collective-permute-start.46) | collective-permute-done | bytes 655392 | tf_op jit(solution)/shard_map/ppermute | solution.py:554
  251.1 6.8 %collective-permute-done.47 = bf16[512,384]{1,0:T(8,128)(2,1)S(1)} collective-permute-done((bf16[512,384]{1,0:T(8,128)(2,1)S(1)}, bf16[512,384]{1,0:T(8,128)(2,1)S(1)}, u32[]{:S(2)}, u32[]{:S(2)}) %collective-permute-start.47) | collective-permute-done | bytes 393248 | tf_op jit(solution)/shard_map/ppermute | solution.py:554
  262.5 9.0 %collective-permute-done.53 = bf16[256,1024]{1,0:T(8,128)(2,1)S(1)} collective-permute-done((bf16[256,1024]{1,0:T(8,128)(2,1)S(1)}, bf16[256,1024]{1,0:T(8,128)(2,1)S(1)}, u32[]{:S(2)}, u32[]{:S(2)}) %collective-permute-start.53) | collective-permute-done | bytes 524320 | tf_op jit(solution)/shard_map/ppermute | solution.py:507
  273.3 2.7 maximum_bitcast_fusion
  276.0 7.0 %collective-permute-done.55 = bf16[512,640]{1,0:T(8,128)(2,1)S(1)} collective-permute-done((bf16[512,640]{1,0:T(8,128)(2,1)S(1)}, bf16[512,640]{1,0:T(8,128)(2,1)S(1)}, u32[]{:S(2)}, u32[]{:S(2)}) %collective-permute-start.55) | collective-permute-done | bytes 655392 | tf_op jit(solution)/shard_map/ppermute | solution.py:554
  284.6 3.7 %collective-permute-done.57 = f32[9,1024]{1,0:T(8,128)S(1)} collective-permute-done((f32[9,1024]{1,0:T(8,128)S(1)}, f32[9,1024]{1,0:T(8,128)S(1)}, u32[]{:S(2)}, u32[]{:S(2)}) %collective-permute-start.57) | collective-permute-done | bytes 36896 | tf_op jit(solution)/shard_map/ppermute | solution.py:624
  295.1 3.2 collective-permute-done.59
  305.3 11.5 %collective-permute-done.56 = bf16[512,640]{1,0:T(8,128)(2,1)S(1)} collective-permute-done((bf16[512,640]{1,0:T(8,128)(2,1)S(1)}, bf16[512,640]{1,0:T(8,128)(2,1)S(1)}, u32[]{:S(2)}, u32[]{:S(2)}) %collective-permute-start.56) | collective-permute-done | bytes 655392 | tf_op jit(solution)/shard_map/ppermute | solution.py:554
  (338 shorter events, 125.5 us)
Async XLA Ops:
  1.2 15.3 %collective-permute-start.1 = (bf16[256,1024]{1,0:T(8,128)(2,1)}, bf16[256,1024]{1,0:T(8,128)(2,1)S(1)}, u32[]{:S(2)}, u32[]{:S(2)}) collective-permute-start(bf16[256,1024]{1,0:T(8,128)(2,1)} %hidden_ref.1), channel_id=1, source_target_pairs={{0,2},{1,3},{2,0},{3,1},{4,6},{5,7},{6,4},{7,5},{8,10},{9,11},{10,... | collective-permute-start | bytes 1572872 | tf_op jit(solution)/shard_map/ppermute | solution.py:507
  16.5 25.7 %collective-permute-start.9 = (bf16[256,1024]{1,0:T(8,128)(2,1)S(1)}, bf16[256,1024]{1,0:T(8,128)(2,1)S(1)}, u32[]{:S(2)}, u32[]{:S(2)}) collective-permute-start(bf16[256,1024]{1,0:T(8,128)(2,1)S(1)} %copy-done.6), channel_id=1, source_target_pairs={{0,1},{1,0},{2,3},{3,2},{4,5},{5,4},{6,7},{7,6},{8,9},{9,8},{10,11... | collective-permute-start | bytes 1572872 | tf_op jit(solution)/shard_map/ppermute | solution.py:507
  29.8 15.0 %collective-permute-start.14 = (bf16[256,1024]{1,0:T(8,128)(2,1)S(1)}, bf16[256,1024]{1,0:T(8,128)(2,1)}, u32[]{:S(2)}, u32[]{:S(2)}) collective-permute-start(bf16[256,1024]{1,0:T(8,128)(2,1)S(1)} %copy-done.15), channel_id=1, source_target_pairs={{0,2},{1,3},{2,0},{3,1},{4,6},{5,7},{6,4},{7,5},{8,10},{9,11},{10,... | collective-permute-start | bytes 1572872 | tf_op jit(solution)/shard_map/ppermute | solution.py:507
  32.1 18.2 %collective-permute-start.5 = (bf16[1024,128]{1,0:T(8,128)(2,1)S(1)}, bf16[1024,128]{1,0:T(8,128)(2,1)}, u32[]{:S(2)}, u32[]{:S(2)}) collective-permute-start(bf16[1024,128]{1,0:T(8,128)(2,1)S(1)} %get-tuple-element.114.refs_0_.context_ref), channel_id=1, source_target_pairs={{0,2},{1,3},{2,0},{3,1},{4,6},{5,7},{6,4},{7,5},{8,10},{9,11},{10,... | collective-permute-start | bytes 786440 | tf_op jit(solution)/shard_map/ppermute | solution.py:507
  95.6 15.1 %collective-permute-start.17 = (bf16[256,1024]{1,0:T(8,128)(2,1)}, bf16[256,1024]{1,0:T(8,128)(2,1)}, u32[]{:S(2)}, u32[]{:S(2)}) collective-permute-start(bf16[256,1024]{1,0:T(8,128)(2,1)} %get-tuple-element.261), channel_id=1, source_target_pairs={{0,4},{4,0},{8,12},{12,8},{16,20},{20,16},{24,28},{28,24},{1,5},{5... | collective-permute-start | bytes 1572872 | tf_op jit(solution)/shard_map/ppermute | solution.py:554
  97.1 20.6 %collective-permute-start.18 = (bf16[256,1024]{1,0:T(8,128)(2,1)}, bf16[256,1024]{1,0:T(8,128)(2,1)S(1)}, u32[]{:S(2)}, u32[]{:S(2)}) collective-permute-start(bf16[256,1024]{1,0:T(8,128)(2,1)} %get-tuple-element.135), channel_id=1, source_target_pairs={{0,1},{1,0},{2,3},{3,2},{4,5},{5,4},{6,7},{7,6},{8,9},{9,8},{10,11... | collective-permute-start | bytes 1572872 | tf_op jit(solution)/shard_map/ppermute | solution.py:507
  99.3 18.5 %collective-permute-start.19 = (bf16[256,1024]{1,0:T(8,128)(2,1)S(1)}, bf16[256,1024]{1,0:T(8,128)(2,1)S(1)}, u32[]{:S(2)}, u32[]{:S(2)}) collective-permute-start(bf16[256,1024]{1,0:T(8,128)(2,1)S(1)} %add_convert_fusion.17), channel_id=1, source_target_pairs={{0,2},{1,3},{2,0},{3,1},{4,6},{5,7},{6,4},{7,5},{8,10},{9,11},{10,... | collective-permute-start | bytes 1572872 | tf_op jit(solution)/shard_map/ppermute | solution.py:507
  102.7 25.9 %collective-permute-start.21 = (bf16[256,1024]{1,0:T(8,128)(2,1)S(1)}, bf16[256,1024]{1,0:T(8,128)(2,1)S(1)}, u32[]{:S(2)}, u32[]{:S(2)}) collective-permute-start(bf16[256,1024]{1,0:T(8,128)(2,1)S(1)} %get-tuple-element.131), channel_id=1, source_target_pairs={{0,4},{4,0},{8,12},{12,8},{16,20},{20,16},{24,28},{28,24},{1,5},{5... | collective-permute-start | bytes 1572872 | tf_op jit(solution)/shard_map/ppermute | solution.py:554
  125.9 19.5 %collective-permute-start.25 = (bf16[256,1024]{1,0:T(8,128)(2,1)S(1)}, bf16[256,1024]{1,0:T(8,128)(2,1)S(1)}, u32[]{:S(2)}, u32[]{:S(2)}) collective-permute-start(bf16[256,1024]{1,0:T(8,128)(2,1)S(1)} %add_convert_fusion.15), channel_id=1, source_target_pairs={{8,16},{12,20},{16,8},{20,12},{9,17},{13,21},{17,9},{21,13},{10,18... | collective-permute-start | bytes 1572872 | tf_op jit(solution)/shard_map/ppermute | solution.py:554
  128.7 18.9 %collective-permute-start.26 = (bf16[256,1024]{1,0:T(8,128)(2,1)S(1)}, bf16[256,1024]{1,0:T(8,128)(2,1)S(1)}, u32[]{:S(2)}, u32[]{:S(2)}) collective-permute-start(bf16[256,1024]{1,0:T(8,128)(2,1)S(1)} %add_convert_fusion.14), channel_id=1, source_target_pairs={{0,8},{4,12},{24,16},{28,20},{1,9},{5,13},{25,17},{29,21},{2,10},{... | collective-permute-start | bytes 1572872 | tf_op jit(solution)/shard_map/ppermute | solution.py:554
  144.3 23.6 %collective-permute-start.33 = (bf16[256,1024]{1,0:T(8,128)(2,1)S(1)}, bf16[256,1024]{1,0:T(8,128)(2,1)}, u32[]{:S(2)}, u32[]{:S(2)}) collective-permute-start(bf16[256,1024]{1,0:T(8,128)(2,1)S(1)} %get-tuple-element.161), channel_id=1, source_target_pairs={{0,2},{1,3},{2,0},{3,1},{4,6},{5,7},{6,4},{7,5},{8,10},{9,11},{10,... | collective-permute-start | bytes 1572872 | tf_op jit(solution)/shard_map/ppermute | solution.py:507
  146.4 22.3 %collective-permute-start.28 = (bf16[256,1024]{1,0:T(8,128)(2,1)}, bf16[256,1024]{1,0:T(8,128)(2,1)}, u32[]{:S(2)}, u32[]{:S(2)}) collective-permute-start(bf16[256,1024]{1,0:T(8,128)(2,1)} %add_convert_fusion.13), channel_id=1, source_target_pairs={{8,0},{12,4},{16,24},{20,28},{9,1},{13,5},{17,25},{21,29},{10,2},{... | collective-permute-start | bytes 1572872 | tf_op jit(solution)/shard_map/ppermute | solution.py:554
  148.7 21.2 %collective-permute-start.29 = (bf16[256,1024]{1,0:T(8,128)(2,1)}, bf16[256,1024]{1,0:T(8,128)(2,1)}, u32[]{:S(2)}, u32[]{:S(2)}) collective-permute-start(bf16[256,1024]{1,0:T(8,128)(2,1)} %add_convert_fusion.12), channel_id=1, source_target_pairs={{8,16},{12,20},{16,8},{20,12},{9,17},{13,21},{17,9},{21,13},{10,18... | collective-permute-start | bytes 1572872 | tf_op jit(solution)/shard_map/ppermute | solution.py:554
  156.9 28.1 %collective-permute-start.32 = (bf16[256,1024]{1,0:T(8,128)(2,1)S(1)}, bf16[256,1024]{1,0:T(8,128)(2,1)}, u32[]{:S(2)}, u32[]{:S(2)}) collective-permute-start(bf16[256,1024]{1,0:T(8,128)(2,1)S(1)} %get-tuple-element.161), channel_id=1, source_target_pairs={{0,1},{1,0},{2,3},{3,2},{4,5},{5,4},{6,7},{7,6},{8,9},{9,8},{10,11... | collective-permute-start | bytes 1572872 | tf_op jit(solution)/shard_map/ppermute | solution.py:507
  159.4 19.0 %collective-permute-start.30 = (bf16[256,1024]{1,0:T(8,128)(2,1)S(1)}, bf16[256,1024]{1,0:T(8,128)(2,1)S(1)}, u32[]{:S(2)}, u32[]{:S(2)}) collective-permute-start(bf16[256,1024]{1,0:T(8,128)(2,1)S(1)} %add_convert_fusion.11), channel_id=1, source_target_pairs={{0,8},{4,12},{24,16},{28,20},{1,9},{5,13},{25,17},{29,21},{2,10},{... | collective-permute-start | bytes 1572872 | tf_op jit(solution)/shard_map/ppermute | solution.py:554
  168.6 20.2 %collective-permute-start.34 = (bf16[256,1024]{1,0:T(8,128)(2,1)}, bf16[256,1024]{1,0:T(8,128)(2,1)S(1)}, u32[]{:S(2)}, u32[]{:S(2)}) collective-permute-start(bf16[256,1024]{1,0:T(8,128)(2,1)} %collective-permute-done.33), channel_id=1, source_target_pairs={{0,1},{1,0},{2,3},{3,2},{4,5},{5,4},{6,7},{7,6},{8,9},{9,8},{10,11... | collective-permute-start | bytes 1572872 | tf_op jit(solution)/shard_map/ppermute | solution.py:507
  171.3 21.5 %collective-permute-start.35 = (bf16[256,1024]{1,0:T(8,128)(2,1)S(1)}, bf16[256,1024]{1,0:T(8,128)(2,1)S(1)}, u32[]{:S(2)}, u32[]{:S(2)}) collective-permute-start(bf16[256,1024]{1,0:T(8,128)(2,1)S(1)} %add_convert_fusion.10), channel_id=1, source_target_pairs={{8,0},{12,4},{16,24},{20,28},{9,1},{13,5},{17,25},{21,29},{10,2},{... | collective-permute-start | bytes 1572872 | tf_op jit(solution)/shard_map/ppermute | solution.py:554
  178.4 15.6 %collective-permute-start.62 = (bf16[256,1024]{1,0:T(8,128)(2,1)S(1)}, bf16[256,1024]{1,0:T(8,128)(2,1)S(1)}, u32[]{:S(2)}, u32[]{:S(2)}) collective-permute-start(bf16[256,1024]{1,0:T(8,128)(2,1)S(1)} %broadcast_select_fusion.6), channel_id=1, source_target_pairs={{0,4},{4,0},{8,12},{12,8},{16,20},{20,16},{24,28},{28,24},{1,5},{5... | collective-permute-start | bytes 1572872 | tf_op jit(solution)/shard_map/ppermute | solution.py:554
  192.9 20.8 %collective-permute-start.63 = (bf16[256,1024]{1,0:T(8,128)(2,1)S(1)}, bf16[256,1024]{1,0:T(8,128)(2,1)S(1)}, u32[]{:S(2)}, u32[]{:S(2)}) collective-permute-start(bf16[256,1024]{1,0:T(8,128)(2,1)S(1)} %broadcast_select_fusion.5), channel_id=1, source_target_pairs={{0,4},{4,0},{8,12},{12,8},{16,20},{20,16},{24,28},{28,24},{1,5},{5... | collective-permute-start | bytes 1572872 | tf_op jit(solution)/shard_map/ppermute | solution.py:554
  194.4 21.9 %collective-permute-start.39 = (bf16[256,1024]{1,0:T(8,128)(2,1)S(1)}, bf16[256,1024]{1,0:T(8,128)(2,1)S(1)}, u32[]{:S(2)}, u32[]{:S(2)}) collective-permute-start(bf16[256,1024]{1,0:T(8,128)(2,1)S(1)} %add_convert_fusion.7), channel_id=1, source_target_pairs={{8,0},{12,4},{16,24},{20,28},{9,1},{13,5},{17,25},{21,29},{10,2},{... | collective-permute-start | bytes 1572872 | tf_op jit(solution)/shard_map/ppermute | solution.py:554
  199.7 16.6 %collective-permute-start.40 = (bf16[256,1024]{1,0:T(8,128)(2,1)S(1)}, bf16[256,1024]{1,0:T(8,128)(2,1)S(1)}, u32[]{:S(2)}, u32[]{:S(2)}) collective-permute-start(bf16[256,1024]{1,0:T(8,128)(2,1)S(1)} %add_convert_fusion.6), channel_id=1, source_target_pairs={{8,16},{12,20},{16,8},{20,12},{9,17},{13,21},{17,9},{21,13},{10,18... | collective-permute-start | bytes 1572872 | tf_op jit(solution)/shard_map/ppermute | solution.py:554
  202.5 15.6 %collective-permute-start.41 = (bf16[512,384]{1,0:T(8,128)(2,1)S(1)}, bf16[512,384]{1,0:T(8,128)(2,1)S(1)}, u32[]{:S(2)}, u32[]{:S(2)}) collective-permute-start(bf16[512,384]{1,0:T(8,128)(2,1)S(1)} %add_convert_fusion.20), channel_id=1, source_target_pairs={{0,8},{4,12},{24,16},{28,20},{1,9},{5,13},{25,17},{29,21},{2,10},{... | collective-permute-start | bytes 1179656 | tf_op jit(solution)/shard_map/ppermute | solution.py:554
  206.8 20.2 %collective-permute-start.42 = (bf16[512,640]{1,0:T(8,128)(2,1)S(1)}, bf16[512,640]{1,0:T(8,128)(2,1)S(1)}, u32[]{:S(2)}, u32[]{:S(2)}) collective-permute-start(bf16[512,640]{1,0:T(8,128)(2,1)S(1)} %get-tuple-element.171), channel_id=1, source_target_pairs={{0,4},{4,0},{8,12},{12,8},{16,20},{20,16},{24,28},{28,24},{1,5},{5... | collective-permute-start | bytes 1966088 | tf_op jit(solution)/shard_map/ppermute | solution.py:554
  216.5 17.2 %collective-permute-start.43 = (bf16[256,1024]{1,0:T(8,128)(2,1)S(1)}, bf16[256,1024]{1,0:T(8,128)(2,1)S(1)}, u32[]{:S(2)}, u32[]{:S(2)}) collective-permute-start(bf16[256,1024]{1,0:T(8,128)(2,1)S(1)} %add_convert_fusion.5), channel_id=1, source_target_pairs={{8,0},{12,4},{16,24},{20,28},{9,1},{13,5},{17,25},{21,29},{10,2},{... | collective-permute-start | bytes 1572872 | tf_op jit(solution)/shard_map/ppermute | solution.py:554
  218.2 15.5 %collective-permute-start.45 = (bf16[512,384]{1,0:T(8,128)(2,1)S(1)}, bf16[512,384]{1,0:T(8,128)(2,1)S(1)}, u32[]{:S(2)}, u32[]{:S(2)}) collective-permute-start(bf16[512,384]{1,0:T(8,128)(2,1)S(1)} %add_convert_fusion.19), channel_id=1, source_target_pairs={{8,16},{12,20},{16,8},{20,12},{9,17},{13,21},{17,9},{21,13},{10,18... | collective-permute-start | bytes 1179656 | tf_op jit(solution)/shard_map/ppermute | solution.py:554
  227.2 16.0 %collective-permute-start.46 = (bf16[512,640]{1,0:T(8,128)(2,1)S(1)}, bf16[512,640]{1,0:T(8,128)(2,1)S(1)}, u32[]{:S(2)}, u32[]{:S(2)}) collective-permute-start(bf16[512,640]{1,0:T(8,128)(2,1)S(1)} %add_convert_fusion.2), channel_id=1, source_target_pairs={{0,8},{4,12},{24,16},{28,20},{1,9},{5,13},{25,17},{29,21},{2,10},{... | collective-permute-start | bytes 1966088 | tf_op jit(solution)/shard_map/ppermute | solution.py:554
  231.1 16.0 %collective-permute-start.48 = (bf16[256,1024]{1,0:T(8,128)(2,1)S(1)}, bf16[256,1024]{1,0:T(8,128)(2,1)S(1)}, u32[]{:S(2)}, u32[]{:S(2)}) collective-permute-start(bf16[256,1024]{1,0:T(8,128)(2,1)S(1)} %get-tuple-element.190), channel_id=1, source_target_pairs={{0,1},{1,0},{2,3},{3,2},{4,5},{5,4},{6,7},{7,6},{8,9},{9,8},{10,11... | collective-permute-start | bytes 1572872 | tf_op jit(solution)/shard_map/ppermute | solution.py:507
  232.5 15.1 %collective-permute-start.49 = (bf16[256,1024]{1,0:T(8,128)(2,1)S(1)}, bf16[256,1024]{1,0:T(8,128)(2,1)S(1)}, u32[]{:S(2)}, u32[]{:S(2)}) collective-permute-start(bf16[256,1024]{1,0:T(8,128)(2,1)S(1)} %add_convert_fusion.4), channel_id=1, source_target_pairs={{0,2},{1,3},{2,0},{3,1},{4,6},{5,7},{6,4},{7,5},{8,10},{9,11},{10,... | collective-permute-start | bytes 1572872 | tf_op jit(solution)/shard_map/ppermute | solution.py:507
  247.6 36.9 %collective-permute-start.65 = (bf16[256,1024]{1,0:T(8,128)(2,1)S(1)}, bf16[256,1024]{1,0:T(8,128)(2,1)S(1)}, u32[]{:S(2)}, u32[]{:S(2)}) collective-permute-start(bf16[256,1024]{1,0:T(8,128)(2,1)S(1)} %broadcast_select_fusion.3), channel_id=1, source_target_pairs={{0,4},{4,0},{8,12},{12,8},{16,20},{20,16},{24,28},{28,24},{1,5},{5... | collective-permute-start | bytes 1572872 | tf_op jit(solution)/shard_map/ppermute | solution.py:554
  259.2 23.8 %collective-permute-start.55 = (bf16[512,640]{1,0:T(8,128)(2,1)S(1)}, bf16[512,640]{1,0:T(8,128)(2,1)S(1)}, u32[]{:S(2)}, u32[]{:S(2)}) collective-permute-start(bf16[512,640]{1,0:T(8,128)(2,1)S(1)} %add_convert_fusion), channel_id=1, source_target_pairs={{8,0},{12,4},{16,24},{20,28},{9,1},{13,5},{17,25},{21,29},{10,2},{... | collective-permute-start | bytes 1966088 | tf_op jit(solution)/shard_map/ppermute | solution.py:554
  261.9 32.1 %collective-permute-start.54 = (bf16[512,384]{1,0:T(8,128)(2,1)S(1)}, bf16[512,384]{1,0:T(8,128)(2,1)}, u32[]{:S(2)}, u32[]{:S(2)}) collective-permute-start(bf16[512,384]{1,0:T(8,128)(2,1)S(1)} %broadcast_select_fusion.17), channel_id=1, source_target_pairs={{0,4},{4,0},{8,12},{12,8},{16,20},{20,16},{24,28},{28,24},{1,5},{5... | collective-permute-start | bytes 1179656 | tf_op jit(solution)/shard_map/ppermute | solution.py:554
  299.6 17.1 %collective-permute-start.56 = (bf16[512,640]{1,0:T(8,128)(2,1)S(1)}, bf16[512,640]{1,0:T(8,128)(2,1)S(1)}, u32[]{:S(2)}, u32[]{:S(2)}) collective-permute-start(bf16[512,640]{1,0:T(8,128)(2,1)S(1)} %broadcast_select_fusion), channel_id=1, source_target_pairs={{0,4},{4,0},{8,12},{12,8},{16,20},{20,16},{24,28},{28,24},{1,5},{5... | collective-permute-start | bytes 1966088 | tf_op jit(solution)/shard_map/ppermute | solution.py:554
  (99 other events, 778.3 us)
